TPU v7x, 256 devices: a whole 4x4x8 slice. The times are simulated.
256 devices in a mesh: gx: 16 (over x_lo, z), gy: 2 (over x_hi), gz: 8 (over y, core).
Axes of the slice: x: 4 (x_hi: 2, x_lo: 2; x = x_hi * 2 + x_lo), y: 4, z: 8, core: 2. Of those that a mesh axis runs over, the one named last changes fastest.
Arguments:
- normed: bfloat16 [1024, 6144], P(('gy', 'gz'), 'gx'), may hold values from -6 to 6
- w_in: bfloat16 [6144, 24576], P('gx', ('gz', 'gy')), may hold values from -0.078125 to 0.078125
- w_out: bfloat16 [24576, 6144], P(('gz', 'gy'), 'gx'), may hold values from -0.0390625 to 0.0390625
- cotangent: bfloat16 [1024, 6144], P(('gy', 'gz'), 'gx'), may hold values from -6 to 6
Outputs:
- block_out: bfloat16 [1024, 6144], P(('gy', 'gz'), 'gx')
- grad_input: bfloat16 [1024, 6144], P(('gy', 'gz'), 'gx')
- grad_w_in: bfloat16 [6144, 24576], P('gx', ('gz', 'gy'))
- grad_w_out: bfloat16 [24576, 6144], P(('gz', 'gy'), 'gx')
All inputs are finite; a program needn't handle non-finite values.
Results may differ from a plain program's by a relative error of at most 0.0049.
Values may be sent and summed in bfloat16 or wider, within the bound.
A program may use at most 128 MiB of HBM per device.

v0:
```python
import math

import jax
import jax.numpy as jnp
from jax import lax
from jax.sharding import PartitionSpec as P


def gelu_value(v):
    return 0.5 * v * (1.0 + jax.scipy.special.erf(v / math.sqrt(2.0)))


def gelu_slope(v):
    return 0.5 * (1.0 + jax.scipy.special.erf(v / math.sqrt(2.0))) + v * jnp.exp(
        -0.5 * v * v
    ) / math.sqrt(2.0 * math.pi)


def contract_first(left, right):
    return lax.dot_general(
        left, right, (((0,), (0,)), ((), ())), preferred_element_type=jnp.float32
    )


def contract_last(left, right):
    return lax.dot_general(
        left, right, (((1,), (1,)), ((), ())), preferred_element_type=jnp.float32
    )


def shards(normed, w_in, w_out, cotangent):
    x_full = lax.all_gather(normed, "gz", axis=0, tiled=True)
    w_in_full = lax.all_gather(w_in, "gy", axis=1, tiled=True)
    preact = lax.psum_scatter(
        jnp.dot(x_full, w_in_full, preferred_element_type=jnp.float32),
        "gx",
        scatter_dimension=0,
        tiled=True,
    )
    hidden = gelu_value(preact).astype(jnp.bfloat16)
    hidden_full = lax.all_gather(hidden, "gx", axis=0, tiled=True)
    w_out_full = lax.all_gather(w_out, "gy", axis=0, tiled=True)
    block_out = lax.psum_scatter(
        jnp.dot(hidden_full, w_out_full, preferred_element_type=jnp.float32),
        "gz",
        scatter_dimension=0,
        tiled=True,
    ).astype(jnp.bfloat16)
    cot_full = lax.all_gather(cotangent, "gz", axis=0, tiled=True)
    grad_hidden = lax.psum_scatter(
        contract_last(cot_full, w_out_full), "gx", scatter_dimension=0, tiled=True
    )
    grad_pre = (grad_hidden * gelu_slope(preact)).astype(jnp.bfloat16)
    grad_full = lax.all_gather(grad_pre, "gx", axis=0, tiled=True)
    grad_input = lax.psum_scatter(
        contract_last(grad_full, w_in_full), "gz", scatter_dimension=0, tiled=True
    ).astype(jnp.bfloat16)
    in_term = contract_first(x_full, grad_full)
    grad_w_in = lax.psum_scatter(in_term, "gy", scatter_dimension=1, tiled=True).astype(
        jnp.bfloat16
    )
    grad_w_out = lax.psum_scatter(
        contract_first(hidden_full, cot_full), "gy", scatter_dimension=0, tiled=True
    ).astype(jnp.bfloat16)
    return (block_out, grad_input, grad_w_in, grad_w_out)


def solution(mesh):
    return jax.shard_map(
        shards,
        mesh=mesh,
        in_specs=(
            P(("gy", "gz"), "gx"),
            P("gx", ("gz", "gy")),
            P(("gz", "gy"), "gx"),
            P(("gy", "gz"), "gx"),
        ),
        out_specs=(
            P(("gy", "gz"), "gx"),
            P(("gy", "gz"), "gx"),
            P("gx", ("gz", "gy")),
            P(("gz", "gy"), "gx"),
        ),
        check_vma=False,
    )
```

profile of v0, /device:TPU:1, one launch (start us, length us, event | category | flops | bytes accessed | tf_op | source)
XLA Modules:
  0.0 639.6 jit_solution(14979726945073501226)
XLA Ops:
  7.2 0.0 all-gather.9.cloned.1.call-start
  7.2 0.7 all-gather.9.cloned.1.call-update
  7.9 0.0 all-gather.5.cloned.1.call-start
  7.9 0.7 all-gather.5.cloned.1.call-update
  8.7 0.0 reduce-scatter.11.cloned.1.call-start
  8.7 16.3 %all_gather.22 = bf16[512,384]{1,0:T(8,128)(2,1)S(1)} all-gather(bf16[64,384]{1,0:T(8,128)(2,1)} %param.7), channel_id=1, replica_groups=mesh['gx'=16,'gy'=2,'gz'=8] {'gz'}, dimensions={0}, use_global_device_ids=true | all-gather | bytes 442368 | tf_op jit(solution)/shard_map/all_gather | solution.py:49
  25.0 31.3 %all-gather.9.cloned.1.call-done = bf16[3072,384]{1,0:T(8,128)(2,1)} async-done(((bf16[1536,384]{1,0:T(8,128)(2,1)}), bf16[3072,384]{1,0:T(8,128)(2,1)}) %all-gather.9.cloned.1.call-update) | async-done | bytes 2359312 | tf_op jit(solution)/shard_map/all_gather | solution.py:42
  56.3 6.2 fusion.8
  62.4 0.0 reduce-scatter.11.cloned.1.call-update
  62.5 0.0 reduce-scatter.7.cloned.1.call-start
  62.5 0.7 copy-done.4
  63.2 13.8 %all_gather.18 = bf16[512,384]{1,0:T(8,128)(2,1)S(1)} all-gather(bf16[64,384]{1,0:T(8,128)(2,1)S(1)} %copy-done.4), channel_id=1, replica_groups=mesh['gx'=16,'gy'=2,'gz'=8] {'gz'}, dimensions={0}, use_global_device_ids=true | all-gather | bytes 442368 | tf_op jit(solution)/shard_map/all_gather | solution.py:32
  77.0 23.2 %all-gather.5.cloned.1.call-done = bf16[384,3072]{1,0:T(8,128)(2,1)} async-done(((bf16[384,1536]{1,0:T(8,128)(2,1)}), bf16[384,3072]{1,0:T(8,128)(2,1)}) %all-gather.5.cloned.1.call-update) | async-done | bytes 2359312 | tf_op jit(solution)/shard_map/all_gather | solution.py:33
  100.2 6.1 fusion.6
  106.3 0.0 copy-done.2
  106.3 0.0 reduce-scatter.7.cloned.1.call-update
  106.4 0.0 all-gather.11.cloned.1.call-start
  106.4 74.7 %reduce-scatter.11.cloned.1.call-done = f32[32,3072]{1,0:T(8,128)} async-done(((f32[512,3072]{1,0:T(8,128)}), f32[32,3072]{1,0:T(8,128)}) %reduce-scatter.11.cloned.1.call-update) | async-done | bytes 393232 | tf_op jit(solution)/shard_map/reduce_scatter | solution.py:50
  181.1 85.6 %reduce-scatter.7.cloned.1.call-done = f32[32,3072]{1,0:T(8,128)} async-done(((f32[512,3072]{1,0:T(8,128)}), f32[32,3072]{1,0:T(8,128)}) %reduce-scatter.7.cloned.1.call-update) | async-done | bytes 393232 | tf_op jit(solution)/shard_map/reduce_scatter | solution.py:34
  266.7 2.0 fusion.5
  268.7 0.0 all-gather.11.cloned.1.call-update
  268.8 0.0 all-gather.7.cloned.1.call-start
  268.8 0.5 all-gather.7.cloned.1.call-update
  269.3 0.0 reduce-scatter.13.cloned.1.call-start
  269.4 70.6 %all-gather.11.cloned.1.call-done = bf16[512,3072]{1,0:T(8,128)(2,1)} async-done(((bf16[32,3072]{1,0:T(8,128)(2,1)}), bf16[512,3072]{1,0:T(8,128)(2,1)}) %all-gather.11.cloned.1.call-update) | async-done | bytes 3145744 | tf_op jit(solution)/shard_map/all_gather | solution.py:54
  340.0 0.0 copy-done.3
  340.0 4.6 fusion.9
  344.6 0.0 reduce-scatter.13.cloned.1.call-update
  344.7 0.0 reduce-scatter.9.cloned.1.call-start
  344.7 69.2 %all-gather.7.cloned.1.call-done = bf16[512,3072]{1,0:T(8,128)(2,1)} async-done(((bf16[32,3072]{1,0:T(8,128)(2,1)}), bf16[512,3072]{1,0:T(8,128)(2,1)}) %all-gather.7.cloned.1.call-update) | async-done | bytes 3145744 | tf_op jit(solution)/shard_map/all_gather | solution.py:41
  413.9 5.3 fusion.7
  419.2 0.0 reduce-scatter.9.cloned.1.call-update
  419.2 0.0 reduce-scatter.15.cloned.1.call-start
  419.3 5.0 convolution_bitcast_fusion
  424.3 0.0 reduce-scatter.15.cloned.1.call-update
  424.3 0.0 reduce-scatter.17.cloned.1.call-start
  424.3 1.8 copy-done
  426.2 4.0 fusion.10
  430.2 0.0 reduce-scatter.17.cloned.1.call-update
  430.2 24.7 %reduce-scatter.13.cloned.1.call-done = f32[64,384]{1,0:T(8,128)} async-done(((f32[512,384]{1,0:T(8,128)}), f32[64,384]{1,0:T(8,128)}) %reduce-scatter.13.cloned.1.call-update) | async-done | bytes 98320 | tf_op jit(solution)/shard_map/reduce_scatter | solution.py:55
  454.9 1.5 convert_element_type.21
  456.4 34.5 %reduce-scatter.9.cloned.1.call-done = f32[64,384]{1,0:T(8,128)} async-done(((f32[512,384]{1,0:T(8,128)}), f32[64,384]{1,0:T(8,128)}) %reduce-scatter.9.cloned.1.call-update) | async-done | bytes 98320 | tf_op jit(solution)/shard_map/reduce_scatter | solution.py:43
  490.9 1.5 convert_element_type.19
  492.4 68.9 %reduce-scatter.15.cloned.1.call-done = f32[384,1536]{0,1:T(8,128)} async-done(((f32[384,3072]{0,1:T(8,128)}), f32[384,1536]{0,1:T(8,128)}) %reduce-scatter.15.cloned.1.call-update) | async-done | bytes 2359312 | tf_op jit(solution)/shard_map/reduce_scatter | solution.py:59
  561.3 1.8 convert_element_type.22
  563.1 1.5 copy.8
  564.6 65.4 %reduce-scatter.17.cloned.1.call-done = f32[1536,384]{1,0:T(8,128)} async-done(((f32[3072,384]{1,0:T(8,128)}), f32[1536,384]{1,0:T(8,128)}) %reduce-scatter.17.cloned.1.call-update) | async-done | bytes 2359312 | tf_op jit(solution)/shard_map/reduce_scatter | solution.py:62
  629.9 2.8 convert_element_type.23
  (6 shorter events, 0.0 us)
Async XLA Ops:
  7.2 49.1 %all-gather.9.cloned.1.call-start = ((), (), s32[]{:S(2)}) async-start(), calls=%async_computation.9 | async-start | bytes 3538944 | tf_op jit(solution)/shard_map/all_gather | solution.py:42
  7.9 92.3 %all-gather.5.cloned.1.call-start = ((), (), s32[]{:S(2)}) async-start(), calls=%async_computation.6 | async-start | bytes 3538944 | tf_op jit(solution)/shard_map/all_gather | solution.py:33
  8.7 172.5 %reduce-scatter.11.cloned.1.call-start = ((), (), s32[]{:S(2)}) async-start(), calls=%async_computation.11 | async-start | bytes 6684672 | tf_op jit(solution)/shard_map/reduce_scatter | solution.py:50
  62.4 0.8 copy-start.4
  62.5 204.2 %reduce-scatter.7.cloned.1.call-start = ((), (), s32[]{:S(2)}) async-start(), calls=%async_computation.7 | async-start | bytes 6684672 | tf_op jit(solution)/shard_map/reduce_scatter | solution.py:34
  77.0 29.3 %copy-start.2 = (bf16[512,384]{1,0:T(8,128)(2,1)}, bf16[512,384]{1,0:T(8,128)(2,1)S(1)}, u32[]{:S(2)}) copy-start(bf16[512,384]{1,0:T(8,128)(2,1)S(1)} %all_gather.18) | copy-start | bytes 1179652
  106.3 233.7 %copy-start.3 = (bf16[384,3072]{1,0:T(8,128)(2,1)S(1)}, bf16[384,3072]{1,0:T(8,128)(2,1)}, u32[]{:S(2)}) copy-start(bf16[384,3072]{1,0:T(8,128)(2,1)} %all-gather.5.cloned.1.call-done) | copy-start | bytes 7077892
  106.4 233.7 %all-gather.11.cloned.1.call-start = ((), (), s32[]{:S(2)}) async-start(), calls=%async_computation.12 | async-start | bytes 3342336 | tf_op jit(solution)/shard_map/all_gather | solution.py:54
  268.8 145.2 %all-gather.7.cloned.1.call-start = ((), (), s32[]{:S(2)}) async-start(), calls=%async_computation.8 | async-start | bytes 3342336 | tf_op jit(solution)/shard_map/all_gather | solution.py:41
  269.3 185.5 %reduce-scatter.13.cloned.1.call-start = ((), (), s32[]{:S(2)}) async-start(), calls=%async_computation.13 | async-start | bytes 884736 | tf_op jit(solution)/shard_map/reduce_scatter | solution.py:55
  344.6 74.7 %copy-start.1 = (bf16[512,3072]{1,0:T(8,128)(2,1)S(1)}, bf16[512,3072]{1,0:T(8,128)(2,1)}, u32[]{:S(2)}) copy-start(bf16[512,3072]{1,0:T(8,128)(2,1)} %all-gather.11.cloned.1.call-done) | copy-start | bytes 9437188
  344.7 146.3 %reduce-scatter.9.cloned.1.call-start = ((), (), s32[]{:S(2)}) async-start(), calls=%async_computation.10 | async-start | bytes 884736 | tf_op jit(solution)/shard_map/reduce_scatter | solution.py:43
  419.2 142.1 %reduce-scatter.15.cloned.1.call-start = ((), (), s32[]{:S(2)}) async-start(), calls=%async_computation.14 | async-start | bytes 7077888 | tf_op jit(solution)/shard_map/reduce_scatter | solution.py:59
  424.3 1.9 copy-start
  424.3 205.7 %reduce-scatter.17.cloned.1.call-start = ((), (), s32[]{:S(2)}) async-start(), calls=%async_computation.15 | async-start | bytes 7077888 | tf_op jit(solution)/shard_map/reduce_scatter | solution.py:62
Sparse Core Ops, SparseCore 0:
  9.8 46.4 all-gather.8
  58.1 42.1 all-gather.4
  102.8 78.2 reduce-scatter.10
  183.5 83.1 reduce-scatter.6
  268.9 71.0 all-gather.10
  341.7 72.2 all-gather.6
  417.0 37.7 reduce-scatter.12
  458.2 32.7 reduce-scatter.8
  493.5 67.8 reduce-scatter.14
  563.9 66.0 reduce-scatter.16
where the time goes:
time: 640 us
  waiting for transfers between devices  550 us (86%)
  matrix products  31.1 us (5%)
  blocking collectives  30.1 us (5%)
  between operations  14.2 us (2%)
  other arithmetic  9.68 us (2%)
    reduce_scatter x1, waiting for transfers between devices, shards(): lax.psum_scatter(jnp.dot(x_full, w_in_full, preferred_element_type=jnp.fl...  85.6 us
    reduce_scatter x1, waiting for transfers between devices, shards(): lax.psum_scatter(contract_last(cot_full, w_out_full), 'gx', scatter_dimen...  74.7 us
    all_gather x1, waiting for transfers between devices, shards(): grad_full = lax.all_gather(grad_pre, 'gx', axis=0, tiled=True)  70.6 us
    all_gather x1, waiting for transfers between devices, shards(): hidden_full = lax.all_gather(hidden, 'gx', axis=0, tiled=True)  69.2 us
    reduce_scatter x1, waiting for transfers between devices, shards(): lax.psum_scatter(in_term, 'gy', scatter_dimension=1, tiled=True)  68.9 us
    reduce_scatter x1, waiting for transfers between devices, shards(): lax.psum_scatter(contract_first(hidden_full, cot_full), 'gy', scatter_dim...  65.4 us
    reduce_scatter x1, waiting for transfers between devices, shards(): lax.psum_scatter(jnp.dot(hidden_full, w_out_full, preferred_element_type=...  34.5 us
    all_gather x1, waiting for transfers between devices, shards(): w_out_full = lax.all_gather(w_out, 'gy', axis=0, tiled=True)  31.3 us
  transfers between devices with their start and end apart: 10, of which 10 were waited for; matrix products, arithmetic and copies ran while one was open for 6% of the time, Pallas kernels for 0%

commit v1 on v0

v1 whole, which is shorter than its diff:
```python
import math

import jax
import jax.numpy as jnp
from jax import lax
from jax.experimental import pallas as pl
from jax.experimental.pallas import tpu as pltpu
from jax.sharding import PartitionSpec as P

BF = jnp.bfloat16
F32 = jnp.float32
MESH = pl.DeviceIdType.MESH

TOK = 1024
CHUNK = 128
DEPTH = 768
UNITS = 768
GROUP = 256
GROUPS = 3
STEPS = ((4, 3), (3, 4))


def gelu_value(v):
    return 0.5 * v * (1.0 + lax.erf(v / math.sqrt(2.0)))


def gelu_slope(v):
    return 0.5 * (1.0 + lax.erf(v / math.sqrt(2.0))) + v * jnp.exp(
        -0.5 * v * v
    ) / math.sqrt(2.0 * math.pi)


def dot(left, right, ldim=1, rdim=0):
    return lax.dot_general(
        left, right, (((ldim,), (rdim,)), ((), ())), preferred_element_type=F32
    )


def kernel(
    normed,
    w_in,
    w_out,
    cot,
    o_block,
    o_gin,
    o_gwin,
    o_gwout,
    acts,
    wi,
    wo,
    hid,
    slope,
    zsend,
    zrecv,
    outp,
    crecv,
    ysend0,
    yrecv0,
    ysend1,
    yrecv1,
    ysum,
    xsend,
    xrecv,
    gw,
    loc_sem,
    ag_send,
    ag_recv,
    w_send,
    w_recv,
    rs_send,
    rs_recv,
    za_send,
    za_recv,
    pl_send,
    pl_recv,
    gw_loc,
    gw_send,
    gw_recv,
):
    gx, gy, gz = lax.axis_index("gx"), lax.axis_index("gy"), lax.axis_index("gz")
    xl, z, xh, y, c = gx // 8, gx % 8, gy, gz // 2, gz % 2
    partner = ((1 - xl) * 8 + z, xh, gz)
    other = ((1 - xl) * 8 + z, 1 - xh, gz)
    zup = (xl * 8 + (z + 1) % 8, xh, gz)
    zdown = (xl * 8 + (z + 7) % 8, xh, gz)
    yup = (gx, xh, ((y + 1) % 4) * 2 + c)
    ydown = (gx, xh, ((y + 3) % 4) * 2 + c)
    sibling = (gx, xh, y * 2 + 1 - c)

    def send(src, dst, ssem, rsem, dev):
        return pltpu.make_async_remote_copy(
            src_ref=src,
            dst_ref=dst,
            send_sem=ssem,
            recv_sem=rsem,
            device_id=dev,
            device_id_type=MESH,
        )

    def arrived(ref, ssem, rsem):
        send(ref, ref, ssem, rsem, sibling).wait_recv()

    def left_here(ref, ssem, rsem):
        send(ref, ref, ssem, rsem, sibling).wait_send()

    def span(start, size, unit=128):
        return pl.ds(pl.multiple_of(start, unit), size)

    def chunk(k):
        return span(k * CHUNK, CHUNK)

    ins = (normed, cot)
    my_rows = span(((c * 4 + y) * 2 + xh) * 64, 64, 64)
    my_cols = span(xl * 384, 384)
    its_cols = span((1 - xl) * 384, 384)
    local = [
        pltpu.make_async_copy(ins[a], acts.at[a, my_rows, my_cols], loc_sem.at[a])
        for a in (0, 1)
    ]
    local.append(
        pltpu.make_async_copy(
            w_in.at[:, span(xl * 768, 768)], wi.at[my_cols, :], loc_sem.at[2]
        )
    )
    local.append(
        pltpu.make_async_copy(
            w_out.at[span(xl * 768, 768), :], wo.at[:, my_cols], loc_sem.at[3]
        )
    )
    for copy in local:
        copy.start()

    barrier = pltpu.get_barrier_semaphore()
    for dev in (partner, other, zup, zdown, yup, ydown, sibling):
        pl.semaphore_signal(barrier, inc=1, device_id=dev, device_id_type=MESH)
    pl.semaphore_wait(barrier, 7)

    def gather_x0(a):
        there = acts.at[a, my_rows, my_cols]
        send(ins[a], there, ag_send.at[a, 0], ag_recv.at[a, 0], partner).start()
        send(ins[a], there, ag_send.at[a, 1], ag_recv.at[a, 1], other).start()

    def gather_x1(a):
        piece = acts.at[a, my_rows, its_cols]
        arrived(piece, ag_send.at[a, 0], ag_recv.at[a, 0])
        send(piece, piece, ag_send.at[a, 2], ag_recv.at[a, 2], other).start()

    def block(a, j):
        return acts.at[a, chunk(c * 4 + (y + j) % 4), :]

    def theirs(a, j):
        return acts.at[a, chunk((1 - c) * 4 + (y + j) % 4), :]

    def half(a, j, h):
        start = (c * 4 + (y + j) % 4) * CHUNK + 64 * h
        return acts.at[a, span(start, 64, 64), :]

    def to_sibling(a, j, slot):
        blk = block(a, j)
        send(blk, blk, ag_send.at[a, slot], ag_recv.at[a, slot], sibling).start()

    def gather_y0(a):
        local[a].wait()
        its_rows = span(((c * 4 + y) * 2 + 1 - xh) * 64, 64, 64)
        arrived(acts.at[a, its_rows, its_cols], ag_send.at[a, 1], ag_recv.at[a, 1])
        arrived(acts.at[a, its_rows, my_cols], ag_send.at[a, 2], ag_recv.at[a, 2])
        blk = block(a, 0)
        send(blk, blk, ag_send.at[a, 3], ag_recv.at[a, 3], yup).start()
        send(blk, blk, ag_send.at[a, 4], ag_recv.at[a, 4], ydown).start()
        to_sibling(a, 0, 7)

    def gather_y1(a):
        arrived(block(a, 3), ag_send.at[a, 3], ag_recv.at[a, 3])
        part = half(a, 3, 0)
        send(part, part, ag_send.at[a, 5], ag_recv.at[a, 5], yup).start()
        arrived(block(a, 1), ag_send.at[a, 4], ag_recv.at[a, 4])
        part = half(a, 1, 1)
        send(part, part, ag_send.at[a, 6], ag_recv.at[a, 6], ydown).start()
        to_sibling(a, 3, 8)
        to_sibling(a, 1, 9)

    def gather_y2(a):
        arrived(half(a, 2, 0), ag_send.at[a, 5], ag_recv.at[a, 5])
        arrived(half(a, 2, 1), ag_send.at[a, 6], ag_recv.at[a, 6])
        to_sibling(a, 2, 10)

    def gather_end(a):
        for slot, j in ((7, 0), (8, 3), (9, 1), (10, 2)):
            arrived(theirs(a, j), ag_send.at[a, slot], ag_recv.at[a, slot])

    def swap_in(g):
        src = w_in.at[:, span((1 - xl) * 768 + g * GROUP, GROUP)]
        dst = wi.at[my_cols, pl.ds(g * GROUP, GROUP)]
        return send(src, dst, w_send.at[0, g], w_recv.at[0, g], partner)

    def swap_out(g):
        src = w_out.at[span((1 - xl) * 768 + g * GROUP, GROUP), :]
        dst = wo.at[pl.ds(g * GROUP, GROUP), my_cols]
        return send(src, dst, w_send.at[1, g], w_recv.at[1, g], partner)

    def group(g):
        return span(g * GROUP, GROUP, GROUP)

    def term(p, g, k):
        if p == 0:
            return dot(acts[0, chunk(k), :], wi[:, group(g)])
        return dot(acts[1, chunk(k), :], wo[group(g), :], 1, 1)

    def each_group(body):
        def step(g, carry):
            body(g)
            return carry

        lax.fori_loop(0, GROUPS, step, 0)

    def reduce_step(p, s):
        up, down = STEPS[p]

        def body(g):
            if s == 0:
                w_arrived(p, g)
            for way, steps, dev in ((0, up, zup), (1, down, zdown)):
                if s >= steps:
                    continue
                slot = s if way == 0 else up + s
                k = (z + up - s) % 8 if way == 0 else (z + 8 - down + s) % 8
                total = term(p, g, k)
                if s > 0:
                    got = zrecv.at[p, g, slot - 1]
                    arrived(got, rs_send.at[p, g, slot - 1], rs_recv.at[p, g, slot - 1])
                    total = total + got[...].astype(F32)
                zsend[p, g, slot] = total.astype(BF)
                send(
                    zsend.at[p, g, slot],
                    zrecv.at[p, g, slot],
                    rs_send.at[p, g, slot],
                    rs_recv.at[p, g, slot],
                    dev,
                ).start()

        each_group(body)

    def w_arrived(p, g):
        if p == 0:
            ref = wi.at[its_cols, group(g)]
        else:
            ref = wo.at[group(g), its_cols]
        arrived(ref, w_send.at[p, g], w_recv.at[p, g])

    def share(p, g, k):
        return hid.at[p, chunk(k), group(g)]

    def hand_on(p, g, k, slot, dev):
        ref = share(p, g, k)
        send(ref, ref, za_send.at[p, g, slot], za_recv.at[p, g, slot], dev).start()

    def reduce_end(p):
        up, down = STEPS[p]

        def body(g):
            total = term(p, g, z)
            for slot in (up - 1, 6):
                got = zrecv.at[p, g, slot]
                arrived(got, rs_send.at[p, g, slot], rs_recv.at[p, g, slot])
                total = total + got[...].astype(F32)
            if p == 0:
                hid[0, chunk(z), group(g)] = gelu_value(total).astype(BF)
                slope[:, group(g)] = gelu_slope(total)
            else:
                hid[1, chunk(z), group(g)] = (total * slope[:, group(g)]).astype(BF)
            hand_on(p, g, z, 0, zup)
            hand_on(p, g, z, up, zdown)

        each_group(body)

    def gather_step(p, s):
        up, down = STEPS[p]

        def body(g):
            for way, steps, dev in ((0, up, zup), (1, down, zdown)):
                if s > steps:
                    continue
                slot = s if way == 0 else up + s
                k = (z + 8 - s) % 8 if way == 0 else (z + s) % 8
                ref = share(p, g, k)
                arrived(ref, za_send.at[p, g, slot - 1], za_recv.at[p, g, slot - 1])
                if s < steps:
                    hand_on(p, g, k, slot, dev)

        each_group(body)

    def out_terms(p):
        def step(k, carry):
            if p == 0:
                outp[0, chunk(k), :] = dot(hid[0, chunk(k), :], wo[...])
            else:
                outp[1, chunk(k), :] = dot(hid[1, chunk(k), :], wi[...], 1, 1)
            return carry

        lax.fori_loop(0, 8, step, 0)

    def plane_core(p):
        send(
            outp.at[p, span((1 - c) * 512, 512), :],
            crecv.at[p],
            pl_send.at[p, 0],
            pl_recv.at[p, 0],
            sibling,
        ).start()

    def own_sum(p, j, h=None):
        q = (y + j) % 4
        start, size, at = c * 512 + q * 128, 128, q * 128
        if h is not None:
            start, size, at = start + 64 * h, 64, at + 64 * h
        return outp[p, span(start, size, 64), :] + crecv[p, span(at, size, 64), :]

    def plane_y0(p):
        arrived(crecv.at[p], pl_send.at[p, 0], pl_recv.at[p, 0])
        for h, dev in ((0, yup), (1, ydown)):
            ysend0[p, h] = own_sum(p, 2, h).astype(BF)
            send(
                ysend0.at[p, h],
                yrecv0.at[p, h],
                pl_send.at[p, 1 + h],
                pl_recv.at[p, 1 + h],
                dev,
            ).start()

    def plane_y1(p):
        for h, dev, j in ((0, yup, 1), (1, ydown, 3)):
            arrived(yrecv0.at[p, h], pl_send.at[p, 1 + h], pl_recv.at[p, 1 + h])
            got = yrecv0[p, h].astype(F32)
            ysend1[p, h, pl.ds(64 * h, 64), :] = (own_sum(p, j, h) + got).astype(BF)
            ysend1[p, h, pl.ds(64 - 64 * h, 64), :] = own_sum(p, j, 1 - h).astype(BF)
            send(
                ysend1.at[p, h],
                yrecv1.at[p, h],
                pl_send.at[p, 3 + h],
                pl_recv.at[p, 3 + h],
                dev,
            ).start()

    def piece(p, dh, dl):
        rows = span(((xh + dh) % 2) * 64, 64, 64)
        return ysum[p, rows, span(((xl + dl) % 2) * 384, 384)]

    def plane_send(p, m, value, dev):
        xsend[p, m] = value
        send(
            xsend.at[p, m],
            xrecv.at[p, m],
            pl_send.at[p, 5 + m],
            pl_recv.at[p, 5 + m],
            dev,
        ).start()

    def plane_x0(p):
        total = own_sum(p, 0)
        for h in (0, 1):
            arrived(yrecv1.at[p, h], pl_send.at[p, 3 + h], pl_recv.at[p, 3 + h])
            total = total + yrecv1[p, h].astype(F32)
        ysum[p] = total
        plane_send(p, 0, piece(p, 1, 0), other)
        plane_send(p, 1, piece(p, 1, 1), other)

    def x_arrived(p, m):
        arrived(xrecv.at[p, m], pl_send.at[p, 5 + m], pl_recv.at[p, 5 + m])
        return xrecv[p, m]

    def plane_x1(p):
        plane_send(p, 2, piece(p, 0, 1) + x_arrived(p, 0), partner)

    def plane_end(p):
        total = piece(p, 0, 0) + x_arrived(p, 1) + x_arrived(p, 2)
        (o_block, o_gin)[p][...] = total.astype(BF)

    def grad_out(g):
        value = dot(hid[0, :, group(g)], acts[1], 0, 0)
        gw[0, group(g), :] = value.astype(BF)
        there = o_gwout.at[span(xl * 768 + g * GROUP, GROUP), :]
        pltpu.make_async_copy(
            gw.at[0, group(g), my_cols], there, gw_loc.at[0, g]
        ).start()
        send(
            gw.at[0, group(g), its_cols],
            there,
            gw_send.at[0, g],
            gw_recv.at[0, g],
            partner,
        ).start()

    def grad_in(g):
        value = dot(acts[0], hid[1, :, group(g)], 0, 0)
        gw[1, :, group(g)] = value.astype(BF)
        there = o_gwin.at[:, span(xl * 768 + g * GROUP, GROUP)]
        pltpu.make_async_copy(
            gw.at[1, my_cols, group(g)], there, gw_loc.at[1, g]
        ).start()
        send(
            gw.at[1, its_cols, group(g)],
            there,
            gw_send.at[1, g],
            gw_recv.at[1, g],
            partner,
        ).start()

    def grads_end():
        def body(g):
            ref = gw.at[0, group(g), its_cols]
            here = o_gwout.at[span((1 - xl) * 768 + g * GROUP, GROUP), :]
            pltpu.make_async_copy(ref, here, gw_loc.at[0, g]).wait()
            left_here(ref, gw_send.at[0, g], gw_recv.at[0, g])
            arrived(here, gw_send.at[0, g], gw_recv.at[0, g])
            ref = gw.at[1, its_cols, group(g)]
            here = o_gwin.at[:, span((1 - xl) * 768 + g * GROUP, GROUP)]
            pltpu.make_async_copy(ref, here, gw_loc.at[1, g]).wait()
            left_here(ref, gw_send.at[1, g], gw_recv.at[1, g])
            arrived(here, gw_send.at[1, g], gw_recv.at[1, g])

        each_group(body)

    def sends_end():
        for a in (0, 1):
            piece_ref = acts.at[a, my_rows, my_cols]
            for slot in (0, 1, 2):
                left_here(piece_ref, ag_send.at[a, slot], ag_recv.at[a, slot])
            for slot in (3, 4, 7, 8, 9, 10):
                left_here(block(a, 0), ag_send.at[a, slot], ag_recv.at[a, slot])
            for slot in (5, 6):
                left_here(half(a, 0, 0), ag_send.at[a, slot], ag_recv.at[a, slot])

        def body(g):
            left_here(wi.at[my_cols, group(g)], w_send.at[0, g], w_recv.at[0, g])
            left_here(wo.at[group(g), my_cols], w_send.at[1, g], w_recv.at[1, g])
            for p in (0, 1):
                for slot in range(7):
                    ref = zsend.at[p, g, slot]
                    left_here(ref, rs_send.at[p, g, slot], rs_recv.at[p, g, slot])
                    ref = share(p, g, z)
                    left_here(ref, za_send.at[p, g, slot], za_recv.at[p, g, slot])

        each_group(body)
        for p in (0, 1):
            left_here(crecv.at[p], pl_send.at[p, 0], pl_recv.at[p, 0])
            for h in (0, 1):
                left_here(ysend0.at[p, h], pl_send.at[p, 1 + h], pl_recv.at[p, 1 + h])
                left_here(ysend1.at[p, h], pl_send.at[p, 3 + h], pl_recv.at[p, 3 + h])
            for m in (0, 1, 2):
                left_here(xsend.at[p, m], pl_send.at[p, 5 + m], pl_recv.at[p, 5 + m])

    gather_x0(0)
    for g in range(GROUPS):
        swap_in(g).start()
    gather_x1(0)
    gather_y0(0)
    gather_x0(1)
    gather_y1(0)
    gather_x1(1)
    for g in range(GROUPS):
        swap_out(g).start()
    gather_y2(0)
    gather_y0(1)
    gather_end(0)
    local[2].wait()
    reduce_step(0, 0)
    gather_y1(1)
    reduce_step(0, 1)
    gather_y2(1)
    reduce_step(0, 2)
    gather_end(1)
    reduce_step(0, 3)
    local[3].wait()
    reduce_step(1, 0)
    reduce_end(0)
    reduce_step(1, 1)
    gather_step(0, 1)
    reduce_step(1, 2)
    gather_step(0, 2)
    reduce_step(1, 3)
    gather_step(0, 3)
    reduce_end(1)
    gather_step(0, 4)
    gather_step(1, 1)
    out_terms(0)
    plane_core(0)
    grad_out(0)
    gather_step(1, 2)
    plane_y0(0)
    grad_out(1)
    plane_y1(0)
    gather_step(1, 3)
    grad_out(2)
    plane_x0(0)
    gather_step(1, 4)
    out_terms(1)
    plane_core(1)
    plane_x1(0)
    grad_in(0)
    plane_y0(1)
    grad_in(1)
    plane_y1(1)
    grad_in(2)
    plane_x0(1)
    plane_end(0)
    plane_x1(1)
    sends_end()
    plane_end(1)
    grads_end()


def shards(normed, w_in, w_out, cotangent):
    hbm = pl.BlockSpec(memory_space=pl.ANY)
    vmem = pl.BlockSpec(memory_space=pltpu.VMEM)
    dma = pltpu.SemaphoreType.DMA
    return pl.pallas_call(
        kernel,
        out_shape=(
            jax.ShapeDtypeStruct((64, 384), BF),
            jax.ShapeDtypeStruct((64, 384), BF),
            jax.ShapeDtypeStruct((384, 1536), BF),
            jax.ShapeDtypeStruct((1536, 384), BF),
        ),
        in_specs=[hbm] * 4,
        out_specs=(vmem, vmem, hbm, hbm),
        scratch_shapes=[
            pltpu.VMEM((2, TOK, DEPTH), BF),
            pltpu.VMEM((DEPTH, UNITS), BF),
            pltpu.VMEM((UNITS, DEPTH), BF),
            pltpu.VMEM((2, TOK, UNITS), BF),
            pltpu.VMEM((CHUNK, UNITS), F32),
            pltpu.VMEM((2, GROUPS, 7, CHUNK, GROUP), BF),
            pltpu.VMEM((2, GROUPS, 7, CHUNK, GROUP), BF),
            pltpu.VMEM((2, TOK, DEPTH), F32),
            pltpu.VMEM((2, 512, DEPTH), F32),
            pltpu.VMEM((2, 2, 64, DEPTH), BF),
            pltpu.VMEM((2, 2, 64, DEPTH), BF),
            pltpu.VMEM((2, 2, CHUNK, DEPTH), BF),
            pltpu.VMEM((2, 2, CHUNK, DEPTH), BF),
            pltpu.VMEM((2, CHUNK, DEPTH), F32),
            pltpu.VMEM((2, 3, 64, 384), F32),
            pltpu.VMEM((2, 3, 64, 384), F32),
            pltpu.VMEM((2, DEPTH, UNITS), BF),
            dma((4,)),
            dma((2, 11)),
            dma((2, 11)),
            dma((2, GROUPS)),
            dma((2, GROUPS)),
            dma((2, GROUPS, 7)),
            dma((2, GROUPS, 7)),
            dma((2, GROUPS, 7)),
            dma((2, GROUPS, 7)),
            dma((2, 8)),
            dma((2, 8)),
            dma((2, GROUPS)),
            dma((2, GROUPS)),
            dma((2, GROUPS)),
        ],
        compiler_params=pltpu.CompilerParams(
            collective_id=0,
            has_side_effects=True,
            vmem_limit_bytes=50 * 1024 * 1024,
        ),
        cost_estimate=pl.CostEstimate(
            flops=7_247_757_312, bytes_accessed=5_000_000, transcendentals=400_000
        ),
    )(normed, w_in, w_out, cotangent)


def solution(mesh):
    return jax.shard_map(
        shards,
        mesh=mesh,
        in_specs=(
            P(("gy", "gz"), "gx"),
            P("gx", ("gz", "gy")),
            P(("gz", "gy"), "gx"),
            P(("gy", "gz"), "gx"),
        ),
        out_specs=(
            P(("gy", "gz"), "gx"),
            P(("gy", "gz"), "gx"),
            P("gx", ("gz", "gy")),
            P(("gz", "gy"), "gx"),
        ),
        check_vma=False,
    )
```

time: 640 us -> 136 us (0.21)
  waiting for transfers between devices: 550 us -> 0 us
  Pallas kernels: 0 us -> 126 us
  matrix products: 31.1 us -> 0 us
  blocking collectives: 30.1 us -> 0 us
  between operations: 14.2 us -> 0.65 us
  other arithmetic: 9.68 us -> 0 us
    reduce_scatter x6 -> x0, waiting for transfers between devices: 354 us -> none  [the longest x1 85.6 us: shards(): lax.psum_scatter(jnp.dot(x_full, w_in_full, preferred_element_type=jnp.fl...]
    all_gather x4 -> x0, waiting for transfers between devices: 194 us -> none  [the longest x1 70.6 us: shards(): grad_full = lax.all_gather(grad_pre, 'gx', axis=0, tiled=True)]
    pallas_call x0 -> x1, Pallas kernels: none -> 126 us  [shards(): pl.pallas_call(kernel, out_shape=(jax.ShapeDtypeStruct((64, 384), BF), ja...]
    dot_general x6 -> x0, matrix products: 31.1 us -> none  [the longest x2 10.7 us: contract_last(): lax.dot_general(left, right, (((1,), (1,)), ((), ())), preferred_element_...]
    all_gather x2 -> x0, blocking collectives: 30.1 us -> none  [the longest x1 16.3 us: shards(): cot_full = lax.all_gather(cotangent, 'gz', axis=0, tiled=True)]
    convert_element_type x5 -> x0, other arithmetic: 9.68 us -> none  [the longest x1 2.81 us: shards(): grad_w_out = lax.psum_scatter(contract_first(hidden_full, cot_full), 'gy'...]
  transfers between devices with their start and end apart: 10 -> 0, of which waited for: 10 -> 0; matrix products, arithmetic and copies ran while one was open for 6% -> 0% of each run, Pallas kernels for 0% -> 0%
where the time goes in v1:
time: 136 us; the launch traced here: 133 us
  Pallas kernels  126 us (93%)
  local copies, waits for them, and re-layouts  6.13 us (5%)
    pallas_call x1, Pallas kernels, shards(): pl.pallas_call(kernel, out_shape=(jax.ShapeDtypeStruct((64, 384), BF), ja...  126 us
    unnamed x10, local copies, waits for them, and re-layouts  6.13 us

profile of v1, /device:TPU:1, one launch (start us, length us, event | category | flops | bytes accessed | tf_op | source)
XLA Modules:
  0.0 133.0 jit_solution(9935380920835412736)
XLA Ops:
  0.6 0.0 copy-start
  0.6 1.3 copy-done
  1.9 0.0 copy-start.1
  1.9 0.8 copy-done.1
  2.7 0.0 copy-start.2
  2.7 0.8 copy-done.2
  3.5 126.3 %shard_map.75 = (bf16[64,384]{1,0:T(8,128)(2,1)S(1)}, bf16[64,384]{1,0:T(8,128)(2,1)S(1)}, bf16[384,1536]{1,0:T(8,128)(2,1)S(1)}, bf16[1536,384]{1,0:T(8,128)(2,1)S(1)}) custom-call(bf16[64,384]{1,0:T(8,128)(2,1)S(1)} %copy-done.1, bf16[384,1536]{1,0:T(8,128)(2,1)S(1)} %copy-done, bf16[1536,384]{1,0:T(8,128)(2,1)} %w_out.1, bf16[64,384]{1,0:T(8,128)(2,1)S(1)} %copy-done.2), custom_call_target="tpu_custom_call" | custom-call | flops 7247757312 | bytes 5000000 | tf_op jit(solution)/shard_map/pallas_call | solution.py:516
  129.8 0.6 copy.12
  130.4 0.6 copy.13
  131.0 1.0 copy.14
  132.0 1.0 copy.15
Async XLA Ops:
  0.6 1.3 copy-start
  1.9 0.8 copy-start.1
  2.7 0.8 copy-start.2

commit v2 on v0

v2 whole, which is shorter than its diff:
```python
import math

import jax
import jax.numpy as jnp
from jax import lax
from jax.experimental import pallas as pl
from jax.experimental.pallas import tpu as pltpu
from jax.sharding import PartitionSpec as P

BF = jnp.bfloat16
F32 = jnp.float32
MESH = pl.DeviceIdType.MESH

TOK = 1024
CHUNK = 128
DEPTH = 768
UNITS = 768
GROUP = 256
GROUPS = 3
STEPS = ((4, 3), (3, 4))
PLACE = (7, 6, 4, 2, 0, 1, 3, 5)


def gelu_value(v):
    return 0.5 * v * (1.0 + lax.erf(v / math.sqrt(2.0)))


def gelu_slope(v):
    return 0.5 * (1.0 + lax.erf(v / math.sqrt(2.0))) + v * jnp.exp(
        -0.5 * v * v
    ) / math.sqrt(2.0 * math.pi)


def dot(left, right, ldim=1, rdim=0):
    return lax.dot_general(
        left, right, (((ldim,), (rdim,)), ((), ())), preferred_element_type=F32
    )


def kernel(
    normed,
    w_in,
    w_out,
    cot,
    o_block,
    o_gin,
    o_gwin,
    o_gwout,
    acts,
    wi,
    wo,
    hid,
    slope,
    zsend,
    zrecv,
    outp,
    crecv,
    ysend,
    yrecv,
    ysum,
    xrecv,
    gw,
    loc_sem,
    wl_sem,
    ag_send,
    ag_recv,
    w_send,
    w_recv,
    rs_send,
    rs_recv,
    za_send,
    za_recv,
    pl_send,
    pl_recv,
    gw_loc,
    gw_send,
    gw_recv,
):
    gx, gy, gz = lax.axis_index("gx"), lax.axis_index("gy"), lax.axis_index("gz")
    xl, z, xh, y, c = gx // 8, gx % 8, gy, gz // 2, gz % 2
    cy = c * 4 + y
    partner = ((1 - xl) * 8 + z, xh, gz)
    other = ((1 - xl) * 8 + z, 1 - xh, gz)
    opposite = (gx, 1 - xh, gz)
    zup = (xl * 8 + (z + 1) % 8, xh, gz)
    zdown = (xl * 8 + (z + 7) % 8, xh, gz)
    ynext = [(gx, xh, ((y + d) % 4) * 2 + c) for d in (1, 2, 3)]
    sibling = (gx, xh, y * 2 + 1 - c)

    def send(src, dst, ssem, rsem, dev):
        return pltpu.make_async_remote_copy(
            src_ref=src,
            dst_ref=dst,
            send_sem=ssem,
            recv_sem=rsem,
            device_id=dev,
            device_id_type=MESH,
        )

    def arrived(ref, ssem, rsem):
        send(ref, ref, ssem, rsem, sibling).wait_recv()

    def left_here(ref, ssem, rsem):
        send(ref, ref, ssem, rsem, sibling).wait_send()

    def span(start, size, unit=128):
        return pl.ds(pl.multiple_of(start, unit), size)

    def group(g):
        return pl.ds(g * GROUP, GROUP)

    ins = (normed, cot)
    my_cols = span(xl * 384, 384)
    its_cols = span((1 - xl) * 384, 384)

    def mine(t):
        b = (z + t + xh) % 2
        return b, span(((z + 4 - t + b * (2 * t + 1)) % 8) // 2 * 16, 16, 16)

    def local_piece(a, t):
        b, rows = mine(t)
        there = acts.at[a, 2 * t + b, cy, :, my_cols]
        return pltpu.make_async_copy(ins[a].at[rows, :], there, loc_sem.at[a, t])

    local_w = (
        pltpu.make_async_copy(
            w_in.at[:, span(xl * 768, 768)], wi.at[my_cols, :], wl_sem.at[0]
        ),
        pltpu.make_async_copy(
            w_out.at[span(xl * 768, 768), :], wo.at[:, my_cols], wl_sem.at[1]
        ),
    )
    for a in (0, 1):
        for t in range(4):
            local_piece(a, t).start()
        local_w[a].start()

    barrier = pltpu.get_barrier_semaphore()
    for dev in (partner, other, opposite, zup, zdown, *ynext, sibling):
        pl.semaphore_signal(barrier, inc=1, device_id=dev, device_id_type=MESH)
    pl.semaphore_wait(barrier, 9)

    def gather_x(a, t):
        b, rows = mine(t)
        there = acts.at[a, 2 * t + b, cy, :, my_cols]
        for m, dev in enumerate((partner, other, opposite)):
            sems = ag_send.at[a, t, m], ag_recv.at[a, t, m]
            send(ins[a].at[rows, :], there, *sems, dev).start()

    def gather_y(a, t):
        b, _ = mine(t)
        local_piece(a, t).wait()
        for m, (q, cols) in enumerate(
            ((b, its_cols), (1 - b, its_cols), (1 - b, my_cols))
        ):
            ref = acts.at[a, 2 * t + q, cy, :, cols]
            arrived(ref, ag_send.at[a, t, m], ag_recv.at[a, t, m])
        ref = acts.at[a, pl.ds(2 * t, 2), cy]
        for d in (0, 2, 1):
            sems = ag_send.at[a, t, 3 + d], ag_recv.at[a, t, 3 + d]
            send(ref, ref, *sems, ynext[d]).start()

    def gather_core(a, t):
        for d in range(3):
            ref = acts.at[a, pl.ds(2 * t, 2), c * 4 + (y + 3 - d) % 4]
            arrived(ref, ag_send.at[a, t, 3 + d], ag_recv.at[a, t, 3 + d])
        ref = acts.at[a, pl.ds(2 * t, 2), pl.ds(c * 4, 4)]
        send(ref, ref, ag_send.at[a, t, 6], ag_recv.at[a, t, 6], sibling).start()

    def gathered(a, t):
        ref = acts.at[a, pl.ds(2 * t, 2), pl.ds((1 - c) * 4, 4)]
        arrived(ref, ag_send.at[a, t, 6], ag_recv.at[a, t, 6])

    def swap_in(g):
        src = w_in.at[:, span((1 - xl) * 768 + g * GROUP, GROUP)]
        dst = wi.at[my_cols, group(g)]
        return send(src, dst, w_send.at[0, g], w_recv.at[0, g], partner)

    def swap_out(g):
        src = w_out.at[span((1 - xl) * 768 + g * GROUP, GROUP), :]
        dst = wo.at[group(g), my_cols]
        return send(src, dst, w_send.at[1, g], w_recv.at[1, g], partner)

    def w_arrived(p, g):
        if p == 0:
            ref = wi.at[its_cols, group(g)]
        else:
            ref = wo.at[group(g), its_cols]
        arrived(ref, w_send.at[p, g], w_recv.at[p, g])

    def term(p, g, slot):
        rows = acts[p, PLACE[slot]].reshape(CHUNK, DEPTH)
        if p == 0:
            return dot(rows, wi[:, group(g)])
        return dot(rows, wo[group(g), :], 1, 1)

    def ways(p):
        up, down = STEPS[p]
        return ((up, 0, zup, 1), (down, up, zdown, -1))

    def reduce_step(p, g, s):
        for steps, first, dev, way in ways(p):
            if s >= steps:
                continue
            n = first + s
            total = term(p, g, way * (steps - s) % 8)
            if s > 0:
                got = zrecv.at[p, g, n - 1]
                sems = rs_send.at[p, g, n - 1], rs_recv.at[p, g, n - 1]
                arrived(got, *sems)
                left_here(got, *sems)
                total = total + got[...].astype(F32)
            zsend[p, g, n] = total.astype(BF)
            sems = rs_send.at[p, g, n], rs_recv.at[p, g, n]
            send(zsend.at[p, g, n], zrecv.at[p, g, n], *sems, dev).start()

    def share(p, g, slot):
        return hid.at[p, PLACE[slot % 8], :, group(g)]

    def reduce_end(p, g):
        total = term(p, g, 0)
        for steps, first, _, _ in ways(p):
            n = first + steps - 1
            got = zrecv.at[p, g, n]
            sems = rs_send.at[p, g, n], rs_recv.at[p, g, n]
            arrived(got, *sems)
            left_here(got, *sems)
            total = total + got[...].astype(F32)
        if p == 0:
            hid[0, PLACE[0], :, group(g)] = gelu_value(total).astype(BF)
            slope[:, group(g)] = gelu_slope(total)
        else:
            value = (total * slope[:, group(g)]).astype(BF)
            hid[1, PLACE[0], :, group(g)] = value
        gather_step(p, g, 0)

    def gather_step(p, g, s):
        for steps, first, dev, way in ways(p):
            if s > steps:
                continue
            n = first + s
            ref = share(p, g, -way * s)
            if s > 0:
                sems = za_send.at[p, g, n - 1], za_recv.at[p, g, n - 1]
                arrived(ref, *sems)
                left_here(ref, *sems)
            if s < steps:
                sems = za_send.at[p, g, n], za_recv.at[p, g, n]
                send(ref, share(p, g, -way * (s + 1)), *sems, dev).start()

    done = {}

    def steps(order):
        for u in order:
            p, g = u // 3, u % 3
            s = done[u] = done.get(u, -1) + 1
            if s == 0:
                w_arrived(p, g)
            if s < 4:
                reduce_step(p, g, s)
            elif s == 4:
                reduce_end(p, g)
            else:
                gather_step(p, g, s - 4)

    def plane_core(p, t):
        rows = hid[p, pl.ds(2 * t, 2)].reshape(2 * CHUNK, UNITS)
        if p == 0:
            value = dot(rows, wo[...])
        else:
            value = dot(rows, wi[...], 1, 1)
        outp[p, t] = value.reshape(2, 8, 16, DEPTH)
        src = outp.at[p, t, :, pl.ds((1 - c) * 4, 4)]
        sems = pl_send.at[p, t, 0], pl_recv.at[p, t, 0]
        send(src, crecv.at[p, t], *sems, sibling).start()

    def plane_y(p, t):
        sems = pl_send.at[p, t, 0], pl_recv.at[p, t, 0]
        arrived(crecv.at[p, t], *sems)
        for d in (0, 2, 1):
            at = (y + 1 + d) % 4
            value = outp[p, t, :, c * 4 + at] + crecv[p, t, :, at]
            ysend[p, t, d] = value.astype(BF)
            sems = pl_send.at[p, t, 1 + d], pl_recv.at[p, t, 1 + d]
            send(ysend.at[p, t, d], yrecv.at[p, t, d], *sems, ynext[d]).start()

    def plane_x(p, t):
        total = outp[p, t, :, cy] + crecv[p, t, :, y]
        for d in range(3):
            sems = pl_send.at[p, t, 1 + d], pl_recv.at[p, t, 1 + d]
            arrived(yrecv.at[p, t, d], *sems)
            total = total + yrecv[p, t, d].astype(F32)
        ysum[p, t] = total
        b, _ = mine(t)
        for m, (q, cols, dev) in enumerate(
            (
                (b, its_cols, partner),
                (1 - b, its_cols, other),
                (1 - b, my_cols, opposite),
            )
        ):
            sems = pl_send.at[p, t, 4 + m], pl_recv.at[p, t, 4 + m]
            src = ysum.at[p, t, q, :, cols]
            send(src, xrecv.at[p, t, m], *sems, dev).start()

    def plane_end(p, t):
        b, rows = mine(t)
        total = ysum[p, t, b, :, my_cols]
        for m in range(3):
            sems = pl_send.at[p, t, 4 + m], pl_recv.at[p, t, 4 + m]
            arrived(xrecv.at[p, t, m], *sems)
            total = total + xrecv[p, t, m]
        (o_block, o_gin)[p][rows, :] = total.astype(BF)

    def grad_out(g):
        left = hid[0, :, :, group(g)].reshape(TOK, GROUP)
        value = dot(left, acts[1].reshape(TOK, DEPTH), 0, 0)
        gw[0, group(g), :] = value.astype(BF)
        there = o_gwout.at[span(xl * 768 + g * GROUP, GROUP), :]
        src = gw.at[0, group(g), its_cols]
        send(src, there, gw_send.at[0, g], gw_recv.at[0, g], partner).start()
        src = gw.at[0, group(g), my_cols]
        pltpu.make_async_copy(src, there, gw_loc.at[0, g]).start()

    def grad_in(g):
        right = hid[1, :, :, group(g)].reshape(TOK, GROUP)
        value = dot(acts[0].reshape(TOK, DEPTH), right, 0, 0)
        gw[1, :, group(g)] = value.astype(BF)
        there = o_gwin.at[:, span(xl * 768 + g * GROUP, GROUP)]
        src = gw.at[1, its_cols, group(g)]
        send(src, there, gw_send.at[1, g], gw_recv.at[1, g], partner).start()
        src = gw.at[1, my_cols, group(g)]
        pltpu.make_async_copy(src, there, gw_loc.at[1, g]).start()

    def grads_end():
        for g in range(GROUPS):
            ref = gw.at[0, group(g), its_cols]
            here = o_gwout.at[span((1 - xl) * 768 + g * GROUP, GROUP), :]
            pltpu.make_async_copy(ref, here, gw_loc.at[0, g]).wait()
            left_here(ref, gw_send.at[0, g], gw_recv.at[0, g])
            arrived(here, gw_send.at[0, g], gw_recv.at[0, g])
            ref = gw.at[1, its_cols, group(g)]
            here = o_gwin.at[:, span((1 - xl) * 768 + g * GROUP, GROUP)]
            pltpu.make_async_copy(ref, here, gw_loc.at[1, g]).wait()
            left_here(ref, gw_send.at[1, g], gw_recv.at[1, g])
            arrived(here, gw_send.at[1, g], gw_recv.at[1, g])

    def inputs_left(a):
        for t in range(4):
            for m in range(3):
                ref = acts.at[a, 0, 0, :, pl.ds(0, 384)]
                left_here(ref, ag_send.at[a, t, m], ag_recv.at[a, t, m])
                ref = acts.at[a, pl.ds(0, 2), 0]
                left_here(ref, ag_send.at[a, t, 3 + m], ag_recv.at[a, t, 3 + m])
            ref = acts.at[a, pl.ds(0, 2), pl.ds(0, 4)]
            left_here(ref, ag_send.at[a, t, 6], ag_recv.at[a, t, 6])

    def weights_left():
        for g in range(GROUPS):
            left_here(wi.at[my_cols, group(g)], w_send.at[0, g], w_recv.at[0, g])
            left_here(wo.at[group(g), my_cols], w_send.at[1, g], w_recv.at[1, g])

    def plane_left(p):
        for t in range(4):
            left_here(crecv.at[p, t], pl_send.at[p, t, 0], pl_recv.at[p, t, 0])
            for d in range(3):
                sems = pl_send.at[p, t, 1 + d], pl_recv.at[p, t, 1 + d]
                left_here(ysend.at[p, t, d], *sems)
                sems = pl_send.at[p, t, 4 + d], pl_recv.at[p, t, 4 + d]
                left_here(xrecv.at[p, t, d], *sems)

    for t in range(4):
        gather_x(0, t)
    swap_in(0).start()
    for t in range(4):
        gather_x(1, t)
    for g in (1, 2):
        swap_in(g).start()
    for g in range(GROUPS):
        swap_out(g).start()
    for t in range(4):
        gather_y(0, t)
    gather_core(0, 0)
    for t in range(4):
        gather_y(1, t)
    local_w[0].wait()
    gather_core(0, 1)
    gathered(0, 0)
    steps((0, 1))
    gather_core(0, 2)
    gathered(0, 1)
    steps((0, 1, 2))
    gather_core(0, 3)
    gathered(0, 2)
    steps((0, 1, 2))
    gather_core(1, 0)
    gather_core(1, 1)
    gathered(0, 3)
    steps((0, 1))
    gather_core(1, 2)
    gather_core(1, 3)
    for t in range(4):
        gathered(1, t)
    local_w[1].wait()
    steps((3, 4, 2, 3, 0, 5, 1, 4, 2, 3, 0, 5, 1, 3, 4, 2, 0, 3, 5, 4, 1, 2, 0))
    inputs_left(0)
    steps((5, 3, 4, 1, 2, 5, 0))
    grad_out(0)
    steps((3, 4, 1))
    grad_out(1)
    steps((2, 5))
    plane_core(0, 3)
    steps((3, 4, 2))
    grad_out(2)
    plane_core(0, 2)
    plane_core(0, 1)
    plane_core(0, 0)
    steps((3,))
    grad_in(0)
    steps((5, 4))
    plane_core(1, 3)
    for t in (3, 2, 1, 0):
        plane_y(0, t)
    plane_core(1, 2)
    steps((5,))
    plane_core(1, 1)
    plane_y(1, 3)
    plane_y(1, 2)
    steps((4,))
    grad_in(1)
    for t in (3, 2, 1, 0):
        plane_x(0, t)
    plane_y(1, 1)
    steps((5,))
    plane_core(1, 0)
    grad_in(2)
    plane_y(1, 0)
    plane_x(1, 3)
    plane_x(1, 2)
    plane_x(1, 1)
    for t in (3, 2, 1, 0):
        plane_end(0, t)
    weights_left()
    inputs_left(1)
    plane_x(1, 0)
    plane_left(0)
    for t in (3, 2, 1, 0):
        plane_end(1, t)
    plane_left(1)
    grads_end()


def shards(normed, w_in, w_out, cotangent):
    hbm = pl.BlockSpec(memory_space=pltpu.HBM)
    vmem = pl.BlockSpec(memory_space=pltpu.VMEM)
    dma = pltpu.SemaphoreType.DMA
    return pl.pallas_call(
        kernel,
        out_shape=(
            jax.ShapeDtypeStruct((64, 384), BF),
            jax.ShapeDtypeStruct((64, 384), BF),
            jax.ShapeDtypeStruct((384, 1536), BF),
            jax.ShapeDtypeStruct((1536, 384), BF),
        ),
        in_specs=[hbm] * 4,
        out_specs=(vmem, vmem, hbm, hbm),
        scratch_shapes=[
            pltpu.VMEM((2, 8, 8, 16, DEPTH), BF),
            pltpu.VMEM((DEPTH, UNITS), BF),
            pltpu.VMEM((UNITS, DEPTH), BF),
            pltpu.VMEM((2, 8, CHUNK, UNITS), BF),
            pltpu.VMEM((CHUNK, UNITS), F32),
            pltpu.VMEM((2, GROUPS, 7, CHUNK, GROUP), BF),
            pltpu.VMEM((2, GROUPS, 7, CHUNK, GROUP), BF),
            pltpu.VMEM((2, 4, 2, 8, 16, DEPTH), F32),
            pltpu.VMEM((2, 4, 2, 4, 16, DEPTH), F32),
            pltpu.VMEM((2, 4, 3, 2, 16, DEPTH), BF),
            pltpu.VMEM((2, 4, 3, 2, 16, DEPTH), BF),
            pltpu.VMEM((2, 4, 2, 16, DEPTH), F32),
            pltpu.VMEM((2, 4, 3, 16, 384), F32),
            pltpu.VMEM((2, DEPTH, UNITS), BF),
            dma((2, 4)),
            dma((2,)),
            dma((2, 4, 7)),
            dma((2, 4, 7)),
            dma((2, GROUPS)),
            dma((2, GROUPS)),
            dma((2, GROUPS, 7)),
            dma((2, GROUPS, 7)),
            dma((2, GROUPS, 7)),
            dma((2, GROUPS, 7)),
            dma((2, 4, 7)),
            dma((2, 4, 7)),
            dma((2, GROUPS)),
            dma((2, GROUPS)),
            dma((2, GROUPS)),
        ],
        compiler_params=pltpu.CompilerParams(
            collective_id=0,
            has_side_effects=True,
            vmem_limit_bytes=58 * 1024 * 1024,
        ),
        cost_estimate=pl.CostEstimate(
            flops=7_247_757_312, bytes_accessed=5_000_000, transcendentals=400_000
        ),
    )(normed, w_in, w_out, cotangent)


def solution(mesh):
    return jax.shard_map(
        shards,
        mesh=mesh,
        in_specs=(
            P(("gy", "gz"), "gx"),
            P("gx", ("gz", "gy")),
            P(("gz", "gy"), "gx"),
            P(("gy", "gz"), "gx"),
        ),
        out_specs=(
            P(("gy", "gz"), "gx"),
            P(("gy", "gz"), "gx"),
            P("gx", ("gz", "gy")),
            P(("gz", "gy"), "gx"),
        ),
        check_vma=False,
    )
```

time: 640 us -> 123 us (0.19)
  waiting for transfers between devices: 550 us -> 0 us
  Pallas kernels: 0 us -> 116 us
  matrix products: 31.1 us -> 0 us
  blocking collectives: 30.1 us -> 0 us
  between operations: 14.2 us -> 0.64 us
  other arithmetic: 9.68 us -> 0 us
    reduce_scatter x6 -> x0, waiting for transfers between devices: 354 us -> none  [the longest x1 85.6 us: shards(): lax.psum_scatter(jnp.dot(x_full, w_in_full, preferred_element_type=jnp.fl...]
    all_gather x4 -> x0, waiting for transfers between devices: 194 us -> none  [the longest x1 70.6 us: shards(): grad_full = lax.all_gather(grad_pre, 'gx', axis=0, tiled=True)]
    pallas_call x0 -> x1, Pallas kernels: none -> 116 us  [shards(): pl.pallas_call(kernel, out_shape=(jax.ShapeDtypeStruct((64, 384), BF), ja...]
    dot_general x6 -> x0, matrix products: 31.1 us -> none  [the longest x2 10.7 us: contract_last(): lax.dot_general(left, right, (((1,), (1,)), ((), ())), preferred_element_...]
    all_gather x2 -> x0, blocking collectives: 30.1 us -> none  [the longest x1 16.3 us: shards(): cot_full = lax.all_gather(cotangent, 'gz', axis=0, tiled=True)]
    convert_element_type x5 -> x0, other arithmetic: 9.68 us -> none  [the longest x1 2.81 us: shards(): grad_w_out = lax.psum_scatter(contract_first(hidden_full, cot_full), 'gy'...]
  transfers between devices with their start and end apart: 10 -> 0, of which waited for: 10 -> 0; matrix products, arithmetic and copies ran while one was open for 6% -> 0% of each run, Pallas kernels for 0% -> 0%
where the time goes in v2:
time: 123 us
  Pallas kernels  116 us (94%)
  local copies, waits for them, and re-layouts  6.32 us (5%)
    pallas_call x1, Pallas kernels, shards(): pl.pallas_call(kernel, out_shape=(jax.ShapeDtypeStruct((64, 384), BF), ja...  116 us
    unnamed x6, local copies, waits for them, and re-layouts  6.32 us

profile of v2, /device:TPU:1, one launch (start us, length us, event | category | flops | bytes accessed | tf_op | source)
XLA Modules:
  0.0 122.8 jit_solution(2178179760731867211)
XLA Ops:
  0.6 115.9 %shard_map.75 = (bf16[64,384]{1,0:T(8,128)(2,1)}, bf16[64,384]{1,0:T(8,128)(2,1)}, bf16[384,1536]{1,0:T(8,128)(2,1)}, bf16[1536,384]{1,0:T(8,128)(2,1)}) custom-call(bf16[64,384]{1,0:T(8,128)(2,1)} %normed.1, bf16[384,1536]{1,0:T(8,128)(2,1)} %w_in.1, bf16[1536,384]{1,0:T(8,128)(2,1)} %w_out.1, bf16[64,384]{1,0:T(8,128)(2,1)} %cot.1), custom_call_target="tpu_custom_call" | custom-call | flops 7247757312 | bytes 5000000 | tf_op jit(solution)/shard_map/pallas_call | solution.py:457
  116.5 1.4 %copy.12 = bf16[64,384]{1,0:T(8,128)(2,1)} copy(bf16[64,384]{1,0:T(8,128)(2,1)} %get-tuple-element.8) | data formatting | bytes 98304
  117.9 1.4 %copy.13 = bf16[64,384]{1,0:T(8,128)(2,1)} copy(bf16[64,384]{1,0:T(8,128)(2,1)} %get-tuple-element.9) | data formatting | bytes 98304
  119.4 0.0 copy-start
  119.4 2.5 %copy.14 = bf16[384,1536]{1,0:T(8,128)(2,1)} copy(bf16[384,1536]{1,0:T(8,128)(2,1)} %get-tuple-element.10) | data formatting | bytes 2359296
  121.8 0.0 copy-done
  121.8 1.0 copy.15
Async XLA Ops:
  119.4 2.5 %copy-start = (bf16[1536,384]{1,0:T(8,128)(2,1)S(1)}, bf16[1536,384]{1,0:T(8,128)(2,1)}, u32[]{:S(2)}) copy-start(bf16[1536,384]{1,0:T(8,128)(2,1)} %get-tuple-element.11) | copy-start | bytes 3538948

commit v3 on v2

--- a/solution.py
+++ b/solution.py
@@ -19,6 +19,118 @@
 GROUPS = 3
 STEPS = ((4, 3), (3, 4))
 PLACE = (7, 6, 4, 2, 0, 1, 3, 5)
+
+
+SCHEDULE = (
+    ("gather_y", 0, 0),
+    ("gather_y", 0, 1),
+    ("gather_y", 0, 2),
+    ("gather_y", 0, 3),
+    ("gather_core", 0, 0),
+    ("reduce", 0, 0, 0),
+    ("gather_y", 1, 0),
+    ("gather_core", 0, 1),
+    ("gather_y", 1, 1),
+    ("gather_y", 1, 2),
+    ("gather_y", 1, 3),
+    ("gather_core", 0, 2),
+    ("reduce", 0, 0, 1),
+    ("gather_core", 0, 3),
+    ("reduce", 0, 1, 0),
+    ("gather_core", 1, 0),
+    ("reduce", 0, 0, 2),
+    ("gather_core", 1, 1),
+    ("reduce", 0, 1, 1),
+    ("reduce", 0, 2, 0),
+    ("gather_core", 1, 2),
+    ("reduce", 0, 0, 3),
+    ("gather_core", 1, 3),
+    ("reduce", 0, 1, 2),
+    ("reduce", 1, 0, 0),
+    ("reduce", 0, 2, 1),
+    ("reduce", 0, 0, 4),
+    ("reduce", 0, 1, 3),
+    ("reduce", 1, 1, 0),
+    ("reduce", 0, 2, 2),
+    ("gather", 0, 0, 1),
+    ("reduce", 0, 1, 4),
+    ("reduce", 1, 2, 0),
+    ("reduce", 0, 2, 3),
+    ("gather", 0, 0, 2),
+    ("gather", 0, 1, 1),
+    ("reduce", 1, 2, 1),
+    ("reduce", 0, 2, 4),
+    ("gather", 0, 0, 3),
+    ("gather", 0, 1, 2),
+    ("reduce", 1, 2, 2),
+    ("reduce", 1, 1, 1),
+    ("gather", 0, 0, 4),
+    ("grad", 0, 0),
+    ("reduce", 1, 0, 1),
+    ("reduce", 1, 2, 3),
+    ("gather", 0, 1, 3),
+    ("gather", 0, 2, 1),
+    ("plane_core", 0, 3),
+    ("reduce", 1, 1, 2),
+    ("plane_y", 0, 3),
+    ("reduce", 1, 2, 4),
+    ("gather", 0, 1, 4),
+    ("grad", 0, 1),
+    ("reduce", 1, 0, 2),
+    ("reduce", 1, 1, 3),
+    ("gather", 0, 2, 2),
+    ("plane_core", 0, 2),
+    ("plane_x", 0, 3),
+    ("gather", 1, 2, 1),
+    ("plane_y", 0, 2),
+    ("reduce", 1, 0, 3),
+    ("reduce", 1, 1, 4),
+    ("gather", 0, 2, 3),
+    ("plane_core", 0, 1),
+    ("plane_end", 0, 3),
+    ("gather", 1, 2, 2),
+    ("plane_x", 0, 2),
+    ("plane_y", 0, 1),
+    ("reduce", 1, 0, 4),
+    ("gather", 1, 1, 1),
+    ("gather", 0, 2, 4),
+    ("grad", 0, 2),
+    ("plane_core", 0, 0),
+    ("plane_end", 0, 2),
+    ("gather", 1, 2, 3),
+    ("plane_x", 0, 1),
+    ("gather", 1, 0, 1),
+    ("plane_core", 1, 3),
+    ("plane_y", 0, 0),
+    ("gather", 1, 1, 2),
+    ("gather", 1, 2, 4),
+    ("grad", 1, 2),
+    ("plane_y", 1, 3),
+    ("gather", 1, 0, 2),
+    ("plane_core", 1, 2),
+    ("plane_x", 0, 0),
+    ("gather", 1, 1, 3),
+    ("plane_end", 0, 1),
+    ("plane_y", 1, 2),
+    ("gather", 1, 0, 3),
+    ("plane_core", 1, 1),
+    ("plane_x", 1, 3),
+    ("gather", 1, 1, 4),
+    ("grad", 1, 1),
+    ("plane_y", 1, 1),
+    ("plane_x", 1, 2),
+    ("gather", 1, 0, 4),
+    ("plane_end", 0, 0),
+    ("plane_core", 1, 0),
+    ("grad", 1, 0),
+    ("plane_end", 1, 3),
+    ("plane_y", 1, 0),
+    ("plane_x", 1, 1),
+    ("plane_end", 1, 2),
+    ("plane_x", 1, 0),
+    ("plane_end", 1, 1),
+    ("plane_end", 1, 0),
+)
 
 
 def gelu_value(v):
@@ -248,20 +360,29 @@
                 sems = za_send.at[p, g, n], za_recv.at[p, g, n]
                 send(ref, share(p, g, -way * (s + 1)), *sems, dev).start()
 
-    done = {}
-
-    def steps(order):
-        for u in order:
-            p, g = u // 3, u % 3
-            s = done[u] = done.get(u, -1) + 1
-            if s == 0:
-                w_arrived(p, g)
-            if s < 4:
-                reduce_step(p, g, s)
-            elif s == 4:
-                reduce_end(p, g)
-            else:
-                gather_step(p, g, s - 4)
+    here = set()
+
+    def need(p, *slots):
+        for slot in slots:
+            t = PLACE[slot % 8] // 2
+            if (p, t) not in here:
+                gathered(p, t)
+                here.add((p, t))
+
+    def reduce(p, g, s):
+        if s == 0:
+            if p not in here:
+                local_w[p].wait()
+                here.add(p)
+            w_arrived(p, g)
+        for steps, _, _, way in ways(p):
+            if s < steps:
+                need(p, way * (steps - s))
+        if s < 4:
+            reduce_step(p, g, s)
+        else:
+            need(p, 0)
+            reduce_end(p, g)
 
     def plane_core(p, t):
         rows = hid[p, pl.ds(2 * t, 2)].reshape(2 * CHUNK, UNITS)
@@ -332,6 +453,10 @@
         src = gw.at[1, my_cols, group(g)]
         pltpu.make_async_copy(src, there, gw_loc.at[1, g]).start()
 
+    def grad(p, g):
+        need(1 - p, *range(8))
+        (grad_out, grad_in)[p](g)
+
     def grads_end():
         for g in range(GROUPS):
             ref = gw.at[0, group(g), its_cols]
@@ -374,94 +499,56 @@
     swap_in(0).start()
     for t in range(4):
         gather_x(1, t)
-    for g in (1, 2):
+    for g in range(1, GROUPS):
         swap_in(g).start()
     for g in range(GROUPS):
         swap_out(g).start()
-    for t in range(4):
-        gather_y(0, t)
-    gather_core(0, 0)
-    for t in range(4):
-        gather_y(1, t)
-    local_w[0].wait()
-    gather_core(0, 1)
-    gathered(0, 0)
-    steps((0, 1))
-    gather_core(0, 2)
-    gathered(0, 1)
-    steps((0, 1, 2))
-    gather_core(0, 3)
-    gathered(0, 2)
-    steps((0, 1, 2))
-    gather_core(1, 0)
-    gather_core(1, 1)
-    gathered(0, 3)
-    steps((0, 1))
-    gather_core(1, 2)
-    gather_core(1, 3)
-    for t in range(4):
-        gathered(1, t)
-    local_w[1].wait()
-    steps((3, 4, 2, 3, 0, 5, 1, 4, 2, 3, 0, 5, 1, 3, 4, 2, 0, 3, 5, 4, 1, 2, 0))
-    inputs_left(0)
-    steps((5, 3, 4, 1, 2, 5, 0))
-    grad_out(0)
-    steps((3, 4, 1))
-    grad_out(1)
-    steps((2, 5))
-    plane_core(0, 3)
-    steps((3, 4, 2))
-    grad_out(2)
-    plane_core(0, 2)
-    plane_core(0, 1)
-    plane_core(0, 0)
-    steps((3,))
-    grad_in(0)
-    steps((5, 4))
-    plane_core(1, 3)
-    for t in (3, 2, 1, 0):
-        plane_y(0, t)
-    plane_core(1, 2)
-    steps((5,))
-    plane_core(1, 1)
-    plane_y(1, 3)
-    plane_y(1, 2)
-    steps((4,))
-    grad_in(1)
-    for t in (3, 2, 1, 0):
-        plane_x(0, t)
-    plane_y(1, 1)
-    steps((5,))
-    plane_core(1, 0)
-    grad_in(2)
-    plane_y(1, 0)
-    plane_x(1, 3)
-    plane_x(1, 2)
-    plane_x(1, 1)
-    for t in (3, 2, 1, 0):
-        plane_end(0, t)
+    table = {
+        "gather_y": gather_y,
+        "gather_core": gather_core,
+        "reduce": reduce,
+        "gather": gather_step,
+        "grad": grad,
+        "plane_core": plane_core,
+        "plane_y": plane_y,
+        "plane_x": plane_x,
+        "plane_end": plane_end,
+    }
+    for name, *where in SCHEDULE:
+        table[name](*where)
     weights_left()
-    inputs_left(1)
-    plane_x(1, 0)
-    plane_left(0)
-    for t in (3, 2, 1, 0):
-        plane_end(1, t)
-    plane_left(1)
+    for a in (0, 1):
+        inputs_left(a)
+        plane_left(a)
     grads_end()
+
+
+def settle(*refs):
+    ins, outs, held, sems = refs[:4], refs[4:8], refs[8:12], refs[12]
+    loads = [pltpu.make_async_copy(ins[i], held[i], sems.at[0, i]) for i in range(4)]
+    stores = [pltpu.make_async_copy(held[i], outs[i], sems.at[1, i]) for i in range(4)]
+    for i in (2, 3, 0, 1):
+        loads[i].start()
+    for i in (2, 3, 0, 1):
+        loads[i].wait()
+        stores[i].start()
+    for store in stores:
+        store.wait()
 
 
 def shards(normed, w_in, w_out, cotangent):
     hbm = pl.BlockSpec(memory_space=pltpu.HBM)
     vmem = pl.BlockSpec(memory_space=pltpu.VMEM)
     dma = pltpu.SemaphoreType.DMA
-    return pl.pallas_call(
+    shapes = (
+        jax.ShapeDtypeStruct((64, 384), BF),
+        jax.ShapeDtypeStruct((64, 384), BF),
+        jax.ShapeDtypeStruct((384, 1536), BF),
+        jax.ShapeDtypeStruct((1536, 384), BF),
+    )
+    results = pl.pallas_call(
         kernel,
-        out_shape=(
-            jax.ShapeDtypeStruct((64, 384), BF),
-            jax.ShapeDtypeStruct((64, 384), BF),
-            jax.ShapeDtypeStruct((384, 1536), BF),
-            jax.ShapeDtypeStruct((1536, 384), BF),
-        ),
+        out_shape=shapes,
         in_specs=[hbm] * 4,
         out_specs=(vmem, vmem, hbm, hbm),
         scratch_shapes=[
@@ -504,6 +591,19 @@
             flops=7_247_757_312, bytes_accessed=5_000_000, transcendentals=400_000
         ),
     )(normed, w_in, w_out, cotangent)
+    return pl.pallas_call(
+        settle,
+        out_shape=shapes,
+        in_specs=[hbm] * 4,
+        out_specs=(hbm,) * 4,
+        scratch_shapes=[
+            *(pltpu.VMEM(shape.shape, BF) for shape in shapes),
+            dma((2, 4)),
+        ],
+        cost_estimate=pl.CostEstimate(
+            flops=0, bytes_accessed=4_900_000, transcendentals=0
+        ),
+    )(*results)
 
 
 def solution(mesh):

time: 123 us -> 112 us (0.911)
  local copies, waits for them, and re-layouts: 6.32 us -> 0 us
  Pallas kernels: 116 us -> 111 us
    unnamed x6 -> x0, local copies, waits for them, and re-layouts: 6.32 us -> none
    pallas_call x1 -> x2, Pallas kernels: 116 us -> 111 us  [the longest x1 108 us: shards(): pl.pallas_call(kernel, out_shape=shapes, in_specs=[hbm] * 4, out_specs=(v...]
where the time goes in v3:
time: 112 us
  Pallas kernels  111 us (99%)
    pallas_call x1, Pallas kernels, shards(): pl.pallas_call(kernel, out_shape=shapes, in_specs=[hbm] * 4, out_specs=(v...  108 us
    pallas_call x1, Pallas kernels, shards(): pl.pallas_call(settle, out_shape=shapes, in_specs=[hbm] * 4, out_specs=(h...  2.76 us

profile of v3, /device:TPU:1, one launch (start us, length us, event | category | flops | bytes accessed | tf_op | source)
XLA Modules:
  0.0 111.9 jit_solution(6831515048689135482)
XLA Ops:
  0.6 108.3 %shard_map.75 = (bf16[64,384]{1,0:T(8,128)(2,1)}, bf16[64,384]{1,0:T(8,128)(2,1)}, bf16[384,1536]{1,0:T(8,128)(2,1)}, bf16[1536,384]{1,0:T(8,128)(2,1)}) custom-call(bf16[64,384]{1,0:T(8,128)(2,1)} %normed.1, bf16[384,1536]{1,0:T(8,128)(2,1)} %w_in.1, bf16[1536,384]{1,0:T(8,128)(2,1)} %w_out.1, bf16[64,384]{1,0:T(8,128)(2,1)} %cot.1), custom_call_target="tpu_custom_call" | custom-call | flops 7247757312 | bytes 5000000 | tf_op jit(solution)/shard_map/pallas_call | solution.py:549
  108.9 2.8 %shard_map.76 = (bf16[64,384]{1,0:T(8,128)(2,1)}, bf16[64,384]{1,0:T(8,128)(2,1)}, bf16[384,1536]{1,0:T(8,128)(2,1)}, bf16[1536,384]{1,0:T(8,128)(2,1)}) custom-call(bf16[64,384]{1,0:T(8,128)(2,1)} %get-tuple-element.8.refs_0_, bf16[64,384]{1,0:T(8,128)(2,1)} %get-tuple-element.9.refs_1_, bf16[384,1536]{1,0:T(8,128)(2,1)} %get-tuple-element.10.refs_2_, ...), custom_call_target="tpu_custom_call" | custom-call | bytes 4900000 | tf_op jit(solution)/shard_map/pallas_call | solution.py:594

commit v4 on v3

--- a/solution.py
+++ b/solution.py
@@ -19,117 +19,144 @@
 GROUPS = 3
 STEPS = ((4, 3), (3, 4))
 PLACE = (7, 6, 4, 2, 0, 1, 3, 5)
-
-
+DIRECT = 0
+
+
+GATHER_Y, GATHER_CORE, REDUCE, GATHER, GRAD = range(5)
+PLANE_CORE, PLANE_Y, PLANE_X, PLANE_X1, PLANE_END = range(5, 10)
 SCHEDULE = (
-    ("gather_y", 0, 0),
-    ("gather_y", 0, 1),
-    ("gather_y", 0, 2),
-    ("gather_y", 0, 3),
-    ("gather_core", 0, 0),
-    ("reduce", 0, 0, 0),
-    ("gather_y", 1, 0),
-    ("gather_core", 0, 1),
-    ("gather_y", 1, 1),
-    ("gather_y", 1, 2),
-    ("gather_y", 1, 3),
-    ("gather_core", 0, 2),
-    ("reduce", 0, 0, 1),
-    ("gather_core", 0, 3),
-    ("reduce", 0, 1, 0),
-    ("gather_core", 1, 0),
-    ("reduce", 0, 0, 2),
-    ("gather_core", 1, 1),
-    ("reduce", 0, 1, 1),
-    ("reduce", 0, 2, 0),
-    ("gather_core", 1, 2),
-    ("reduce", 0, 0, 3),
-    ("gather_core", 1, 3),
-    ("reduce", 0, 1, 2),
-    ("reduce", 1, 0, 0),
-    ("reduce", 0, 2, 1),
-    ("reduce", 0, 0, 4),
-    ("reduce", 0, 1, 3),
-    ("reduce", 1, 1, 0),
-    ("reduce", 0, 2, 2),
-    ("gather", 0, 0, 1),
-    ("reduce", 0, 1, 4),
-    ("reduce", 1, 2, 0),
-    ("reduce", 0, 2, 3),
-    ("gather", 0, 0, 2),
-    ("gather", 0, 1, 1),
-    ("reduce", 1, 2, 1),
-    ("reduce", 0, 2, 4),
-    ("gather", 0, 0, 3),
-    ("gather", 0, 1, 2),
-    ("reduce", 1, 2, 2),
-    ("reduce", 1, 1, 1),
-    ("gather", 0, 0, 4),
-    ("grad", 0, 0),
-    ("reduce", 1, 0, 1),
-    ("reduce", 1, 2, 3),
-    ("gather", 0, 1, 3),
-    ("gather", 0, 2, 1),
-    ("plane_core", 0, 3),
-    ("reduce", 1, 1, 2),
-    ("plane_y", 0, 3),
-    ("reduce", 1, 2, 4),
-    ("gather", 0, 1, 4),
-    ("grad", 0, 1),
-    ("reduce", 1, 0, 2),
-    ("reduce", 1, 1, 3),
-    ("gather", 0, 2, 2),
-    ("plane_core", 0, 2),
-    ("plane_x", 0, 3),
-    ("gather", 1, 2, 1),
-    ("plane_y", 0, 2),
-    ("reduce", 1, 0, 3),
-    ("reduce", 1, 1, 4),
-    ("gather", 0, 2, 3),
-    ("plane_core", 0, 1),
-    ("plane_end", 0, 3),
-    ("gather", 1, 2, 2),
-    ("plane_x", 0, 2),
-    ("plane_y", 0, 1),
-    ("reduce", 1, 0, 4),
-    ("gather", 1, 1, 1),
-    ("gather", 0, 2, 4),
-    ("grad", 0, 2),
-    ("plane_core", 0, 0),
-    ("plane_end", 0, 2),
-    ("gather", 1, 2, 3),
-    ("plane_x", 0, 1),
-    ("gather", 1, 0, 1),
-    ("plane_core", 1, 3),
-    ("plane_y", 0, 0),
-    ("gather", 1, 1, 2),
-    ("gather", 1, 2, 4),
-    ("grad", 1, 2),
-    ("plane_y", 1, 3),
-    ("gather", 1, 0, 2),
-    ("plane_core", 1, 2),
-    ("plane_x", 0, 0),
-    ("gather", 1, 1, 3),
-    ("plane_end", 0, 1),
-    ("plane_y", 1, 2),
-    ("gather", 1, 0, 3),
-    ("plane_core", 1, 1),
-    ("plane_x", 1, 3),
-    ("gather", 1, 1, 4),
-    ("grad", 1, 1),
-    ("plane_y", 1, 1),
-    ("plane_x", 1, 2),
-    ("gather", 1, 0, 4),
-    ("plane_end", 0, 0),
-    ("plane_core", 1, 0),
-    ("grad", 1, 0),
-    ("plane_end", 1, 3),
-    ("plane_y", 1, 0),
-    ("plane_x", 1, 1),
-    ("plane_end", 1, 2),
-    ("plane_x", 1, 0),
-    ("plane_end", 1, 1),
-    ("plane_end", 1, 0),
+    (GATHER_Y, 0, 0),
+    (GATHER_Y, 0, 1),
+    (GATHER_Y, 0, 2),
+    (GATHER_Y, 0, 3),
+    (GATHER_CORE, 0, 0),
+    (REDUCE, 0, 0, 0),
+    (GATHER_Y, 1, 1),
+    (GATHER_CORE, 0, 1),
+    (REDUCE, 0, 0, 1),
+    (GATHER_Y, 1, 0),
+    (GATHER_CORE, 0, 2),
+    (REDUCE, 0, 1, 0),
+    (GATHER_Y, 1, 3),
+    (REDUCE, 0, 0, 2),
+    (GATHER_CORE, 0, 3),
+    (GATHER_CORE, 1, 1),
+    (REDUCE, 0, 1, 1),
+    (REDUCE, 0, 2, 0),
+    (REDUCE, 0, 0, 3),
+    (REDUCE, 0, 1, 2),
+    (GATHER_Y, 1, 2),
+    (REDUCE, 0, 2, 1),
+    (GATHER_CORE, 1, 0),
+    (REDUCE, 0, 0, 4),
+    (GATHER_CORE, 1, 3),
+    (REDUCE, 1, 0, 0),
+    (REDUCE, 0, 2, 2),
+    (GATHER, 0, 0, 1),
+    (GATHER_CORE, 1, 2),
+    (REDUCE, 0, 1, 3),
+    (REDUCE, 1, 1, 0),
+    (REDUCE, 0, 2, 3),
+    (REDUCE, 1, 2, 0),
+    (REDUCE, 0, 1, 4),
+    (REDUCE, 0, 2, 4),
+    (REDUCE, 1, 0, 1),
+    (REDUCE, 1, 2, 1),
+    (GATHER, 0, 0, 2),
+    (GATHER, 0, 2, 1),
+    (GATHER, 0, 1, 1),
+    (REDUCE, 1, 2, 2),
+    (GATHER, 0, 0, 3),
+    (REDUCE, 1, 0, 2),
+    (REDUCE, 1, 1, 1),
+    (PLANE_CORE, 0, 3, 0),
+    (GATHER, 0, 2, 2),
+    (REDUCE, 1, 0, 3),
+    (GATHER, 0, 1, 2),
+    (GATHER, 0, 0, 4),
+    (PLANE_CORE, 0, 2, 1),
+    (PLANE_Y, 0, 3, 0),
+    (PLANE_CORE, 0, 1, 1),
+    (PLANE_CORE, 0, 3, 1),
+    (GRAD, 0, 0),
+    (REDUCE, 1, 1, 2),
+    (REDUCE, 1, 0, 4),
+    (REDUCE, 1, 2, 3),
+    (PLANE_CORE, 0, 2, 0),
+    (PLANE_Y, 0, 3, 1),
+    (GATHER, 0, 2, 3),
+    (PLANE_Y, 0, 2, 0),
+    (GATHER, 0, 1, 3),
+    (REDUCE, 1, 1, 3),
+    (PLANE_Y, 0, 1, 1),
+    (PLANE_CORE, 0, 1, 0),
+    (GATHER, 1, 0, 1),
+    (PLANE_Y, 0, 2, 1),
+    (REDUCE, 1, 2, 4),
+    (GATHER, 0, 2, 4),
+    (GRAD, 0, 2),
+    (PLANE_Y, 0, 1, 0),
+    (GATHER, 0, 1, 4),
+    (REDUCE, 1, 1, 4),
+    (PLANE_CORE, 0, 0, 1),
+    (GRAD, 0, 1),
+    (GATHER, 1, 0, 2),
+    (PLANE_X, 0, 3),
+    (PLANE_CORE, 0, 0, 0),
+    (GATHER, 1, 2, 1),
+    (PLANE_Y, 0, 0, 1),
+    (PLANE_Y, 0, 0, 0),
+    (GATHER, 1, 1, 1),
+    (PLANE_CORE, 1, 3, 1),
+    (PLANE_X, 0, 2),
+    (PLANE_X, 0, 1),
+    (PLANE_CORE, 1, 3, 0),
+    (GATHER, 1, 0, 3),
+    (GATHER, 1, 2, 2),
+    (PLANE_CORE, 1, 2, 1),
+    (PLANE_X1, 0, 3),
+    (PLANE_X1, 0, 2),
+    (GATHER, 1, 1, 2),
+    (PLANE_CORE, 1, 1, 1),
+    (PLANE_X1, 0, 1),
+    (PLANE_Y, 1, 3, 1),
+    (PLANE_Y, 1, 2, 1),
+    (GATHER, 1, 0, 4),
+    (GRAD, 1, 0),
+    (PLANE_CORE, 1, 2, 0),
+    (GATHER, 1, 2, 3),
+    (PLANE_Y, 1, 1, 1),
+    (PLANE_X, 0, 0),
+    (PLANE_Y, 1, 3, 0),
+    (PLANE_END, 0, 1),
+    (GATHER, 1, 1, 3),
+    (PLANE_Y, 1, 2, 0),
+    (PLANE_CORE, 1, 1, 0),
+    (PLANE_CORE, 1, 0, 1),
+    (PLANE_X1, 0, 0),
+    (GATHER, 1, 2, 4),
+    (GRAD, 1, 2),
+    (PLANE_Y, 1, 1, 0),
+    (PLANE_X, 1, 3),
+    (GATHER, 1, 1, 4),
+    (PLANE_CORE, 1, 0, 0),
+    (PLANE_Y, 1, 0, 1),
+    (PLANE_X, 1, 2),
+    (PLANE_END, 0, 0),
+    (PLANE_Y, 1, 0, 0),
+    (PLANE_X, 1, 1),
+    (PLANE_X1, 1, 3),
+    (PLANE_END, 0, 3),
+    (GRAD, 1, 1),
+    (PLANE_X1, 1, 2),
+    (PLANE_X, 1, 0),
+    (PLANE_X1, 1, 1),
+    (PLANE_END, 1, 3),
+    (PLANE_X1, 1, 0),
+    (PLANE_END, 1, 1),
+    (PLANE_END, 0, 2),
+    (PLANE_END, 1, 2),
+    (PLANE_END, 1, 0),
 )
 
 
@@ -170,6 +197,7 @@
     ysend,
     yrecv,
     ysum,
+    xsend,
     xrecv,
     gw,
     loc_sem,
@@ -253,15 +281,15 @@
     pl.semaphore_wait(barrier, 9)
 
     def gather_x(a, t):
-        b, rows = mine(t)
+        b, _ = mine(t)
         there = acts.at[a, 2 * t + b, cy, :, my_cols]
+        local_piece(a, t).wait()
         for m, dev in enumerate((partner, other, opposite)):
             sems = ag_send.at[a, t, m], ag_recv.at[a, t, m]
-            send(ins[a].at[rows, :], there, *sems, dev).start()
+            send(there, there, *sems, dev).start()
 
     def gather_y(a, t):
         b, _ = mine(t)
-        local_piece(a, t).wait()
         for m, (q, cols) in enumerate(
             ((b, its_cols), (1 - b, its_cols), (1 - b, my_cols))
         ):
@@ -306,12 +334,12 @@
             return dot(rows, wi[:, group(g)])
         return dot(rows, wo[group(g), :], 1, 1)
 
-    def ways(p):
-        up, down = STEPS[p]
+    def ways(p, g):
+        up, down = STEPS[(p + g) % 2]
         return ((up, 0, zup, 1), (down, up, zdown, -1))
 
     def reduce_step(p, g, s):
-        for steps, first, dev, way in ways(p):
+        for steps, first, dev, way in ways(p, g):
             if s >= steps:
                 continue
             n = first + s
@@ -331,7 +359,7 @@
 
     def reduce_end(p, g):
         total = term(p, g, 0)
-        for steps, first, _, _ in ways(p):
+        for steps, first, _, _ in ways(p, g):
             n = first + steps - 1
             got = zrecv.at[p, g, n]
             sems = rs_send.at[p, g, n], rs_recv.at[p, g, n]
@@ -347,7 +375,7 @@
         gather_step(p, g, 0)
 
     def gather_step(p, g, s):
-        for steps, first, dev, way in ways(p):
+        for steps, first, dev, way in ways(p, g):
             if s > steps:
                 continue
             n = first + s
@@ -375,7 +403,7 @@
                 local_w[p].wait()
                 here.add(p)
             w_arrived(p, g)
-        for steps, _, _, way in ways(p):
+        for steps, _, _, way in ways(p, g):
             if s < steps:
                 need(p, way * (steps - s))
         if s < 4:
@@ -384,53 +412,70 @@
             need(p, 0)
             reduce_end(p, g)
 
-    def plane_core(p, t):
-        rows = hid[p, pl.ds(2 * t, 2)].reshape(2 * CHUNK, UNITS)
+    def plane_core(p, t, h):
+        rows = hid[p, 2 * t + h]
         if p == 0:
             value = dot(rows, wo[...])
         else:
             value = dot(rows, wi[...], 1, 1)
-        outp[p, t] = value.reshape(2, 8, 16, DEPTH)
-        src = outp.at[p, t, :, pl.ds((1 - c) * 4, 4)]
-        sems = pl_send.at[p, t, 0], pl_recv.at[p, t, 0]
-        send(src, crecv.at[p, t], *sems, sibling).start()
-
-    def plane_y(p, t):
-        sems = pl_send.at[p, t, 0], pl_recv.at[p, t, 0]
-        arrived(crecv.at[p, t], *sems)
+        outp[p, t, h] = value.reshape(8, 16, DEPTH)
+        src = outp.at[p, t, h, pl.ds((1 - c) * 4, 4)]
+        sems = pl_send.at[p, t, h], pl_recv.at[p, t, h]
+        send(src, crecv.at[p, t, h], *sems, sibling).start()
+
+    def plane_y(p, t, h):
+        sems = pl_send.at[p, t, h], pl_recv.at[p, t, h]
+        arrived(crecv.at[p, t, h], *sems)
         for d in (0, 2, 1):
             at = (y + 1 + d) % 4
-            value = outp[p, t, :, c * 4 + at] + crecv[p, t, :, at]
-            ysend[p, t, d] = value.astype(BF)
-            sems = pl_send.at[p, t, 1 + d], pl_recv.at[p, t, 1 + d]
-            send(ysend.at[p, t, d], yrecv.at[p, t, d], *sems, ynext[d]).start()
+            value = outp[p, t, h, c * 4 + at] + crecv[p, t, h, at]
+            ysend[p, t, d, h] = value.astype(BF)
+            n = 2 + 3 * h + d
+            sems = pl_send.at[p, t, n], pl_recv.at[p, t, n]
+            send(ysend.at[p, t, d, h], yrecv.at[p, t, d, h], *sems, ynext[d]).start()
 
     def plane_x(p, t):
         total = outp[p, t, :, cy] + crecv[p, t, :, y]
         for d in range(3):
-            sems = pl_send.at[p, t, 1 + d], pl_recv.at[p, t, 1 + d]
-            arrived(yrecv.at[p, t, d], *sems)
+            for h in (0, 1):
+                n = 2 + 3 * h + d
+                sems = pl_send.at[p, t, n], pl_recv.at[p, t, n]
+                arrived(yrecv.at[p, t, d, h], *sems)
             total = total + yrecv[p, t, d].astype(F32)
         ysum[p, t] = total
         b, _ = mine(t)
         for m, (q, cols, dev) in enumerate(
             (
+                (1 - b, my_cols, opposite if direct(p, t) else other),
+                (1 - b, its_cols, other),
                 (b, its_cols, partner),
-                (1 - b, its_cols, other),
-                (1 - b, my_cols, opposite),
             )
         ):
-            sems = pl_send.at[p, t, 4 + m], pl_recv.at[p, t, 4 + m]
-            src = ysum.at[p, t, q, :, cols]
-            send(src, xrecv.at[p, t, m], *sems, dev).start()
+            if m < 2 or direct(p, t):
+                x_send(p, t, m, ysum.at[p, t, q, :, cols], dev)
+
+    def direct(p, t):
+        return p == 1 and t < DIRECT
+
+    def x_send(p, t, m, src, dev):
+        sems = pl_send.at[p, t, 8 + m], pl_recv.at[p, t, 8 + m]
+        send(src, xrecv.at[p, t, m], *sems, dev).start()
+
+    def x_arrived(p, t, m):
+        sems = pl_send.at[p, t, 8 + m], pl_recv.at[p, t, 8 + m]
+        arrived(xrecv.at[p, t, m], *sems)
+        return xrecv[p, t, m]
+
+    def plane_x1(p, t):
+        b, _ = mine(t)
+        xsend[p, t] = ysum[p, t, b, :, its_cols] + x_arrived(p, t, 0)
+        x_send(p, t, 2, xsend.at[p, t], partner)
 
     def plane_end(p, t):
         b, rows = mine(t)
         total = ysum[p, t, b, :, my_cols]
-        for m in range(3):
-            sems = pl_send.at[p, t, 4 + m], pl_recv.at[p, t, 4 + m]
-            arrived(xrecv.at[p, t, m], *sems)
-            total = total + xrecv[p, t, m]
+        for m in (0, 1, 2) if direct(p, t) else (1, 2):
+            total = total + x_arrived(p, t, m)
         (o_block, o_gin)[p][rows, :] = total.astype(BF)
 
     def grad_out(g):
@@ -487,12 +532,16 @@
 
     def plane_left(p):
         for t in range(4):
-            left_here(crecv.at[p, t], pl_send.at[p, t, 0], pl_recv.at[p, t, 0])
-            for d in range(3):
-                sems = pl_send.at[p, t, 1 + d], pl_recv.at[p, t, 1 + d]
-                left_here(ysend.at[p, t, d], *sems)
-                sems = pl_send.at[p, t, 4 + d], pl_recv.at[p, t, 4 + d]
-                left_here(xrecv.at[p, t, d], *sems)
+            for h in (0, 1):
+                sems = pl_send.at[p, t, h], pl_recv.at[p, t, h]
+                left_here(crecv.at[p, t, h], *sems)
+                for d in range(3):
+                    n = 2 + 3 * h + d
+                    sems = pl_send.at[p, t, n], pl_recv.at[p, t, n]
+                    left_here(ysend.at[p, t, d, h], *sems)
+            for m in range(3):
+                sems = pl_send.at[p, t, 8 + m], pl_recv.at[p, t, 8 + m]
+                left_here(xrecv.at[p, t, m], *sems)
 
     for t in range(4):
         gather_x(0, t)
@@ -504,18 +553,19 @@
     for g in range(GROUPS):
         swap_out(g).start()
     table = {
-        "gather_y": gather_y,
-        "gather_core": gather_core,
-        "reduce": reduce,
-        "gather": gather_step,
-        "grad": grad,
-        "plane_core": plane_core,
-        "plane_y": plane_y,
-        "plane_x": plane_x,
-        "plane_end": plane_end,
+        GATHER_Y: gather_y,
+        GATHER_CORE: gather_core,
+        REDUCE: reduce,
+        GATHER: gather_step,
+        GRAD: grad,
+        PLANE_CORE: plane_core,
+        PLANE_Y: plane_y,
+        PLANE_X: plane_x,
+        PLANE_X1: plane_x1,
+        PLANE_END: plane_end,
     }
-    for name, *where in SCHEDULE:
-        table[name](*where)
+    for what, *where in SCHEDULE:
+        table[what](*where)
     weights_left()
     for a in (0, 1):
         inputs_left(a)
@@ -564,6 +614,7 @@
             pltpu.VMEM((2, 4, 3, 2, 16, DEPTH), BF),
             pltpu.VMEM((2, 4, 3, 2, 16, DEPTH), BF),
             pltpu.VMEM((2, 4, 2, 16, DEPTH), F32),
+            pltpu.VMEM((2, 4, 16, 384), F32),
             pltpu.VMEM((2, 4, 3, 16, 384), F32),
             pltpu.VMEM((2, DEPTH, UNITS), BF),
             dma((2, 4)),
@@ -576,8 +627,8 @@
             dma((2, GROUPS, 7)),
             dma((2, GROUPS, 7)),
             dma((2, GROUPS, 7)),
-            dma((2, 4, 7)),
-            dma((2, 4, 7)),
+            dma((2, 4, 11)),
+            dma((2, 4, 11)),
             dma((2, GROUPS)),
             dma((2, GROUPS)),
             dma((2, GROUPS)),

time: 112 us -> 110 us (0.982)
  Pallas kernels: 111 us -> 109 us
    pallas_call x1, Pallas kernels: 108 us -> 106 us  [shards(): pl.pallas_call(kernel, out_shape=shapes, in_specs=[hbm] * 4, out_specs=(v...]
where the time goes in v4:
time: 110 us
  Pallas kernels  109 us (99%)
    pallas_call x1, Pallas kernels, shards(): pl.pallas_call(kernel, out_shape=shapes, in_specs=[hbm] * 4, out_specs=(v...  106 us
    pallas_call x1, Pallas kernels, shards(): pl.pallas_call(settle, out_shape=shapes, in_specs=[hbm] * 4, out_specs=(h...  2.76 us

profile of v4, /device:TPU:1, one launch (start us, length us, event | category | flops | bytes accessed | tf_op | source)
XLA Modules:
  0.0 110.0 jit_solution(8947695840867159548)
XLA Ops:
  0.6 106.5 %shard_map.75 = (bf16[64,384]{1,0:T(8,128)(2,1)}, bf16[64,384]{1,0:T(8,128)(2,1)}, bf16[384,1536]{1,0:T(8,128)(2,1)}, bf16[1536,384]{1,0:T(8,128)(2,1)}) custom-call(bf16[64,384]{1,0:T(8,128)(2,1)} %normed.1, bf16[384,1536]{1,0:T(8,128)(2,1)} %w_in.1, bf16[1536,384]{1,0:T(8,128)(2,1)} %w_out.1, bf16[64,384]{1,0:T(8,128)(2,1)} %cot.1), custom_call_target="tpu_custom_call" | custom-call | flops 7247757312 | bytes 5000000 | tf_op jit(solution)/shard_map/pallas_call | solution.py:599
  107.1 2.8 %shard_map.76 = (bf16[64,384]{1,0:T(8,128)(2,1)}, bf16[64,384]{1,0:T(8,128)(2,1)}, bf16[384,1536]{1,0:T(8,128)(2,1)}, bf16[1536,384]{1,0:T(8,128)(2,1)}) custom-call(bf16[64,384]{1,0:T(8,128)(2,1)} %get-tuple-element.8.refs_0_, bf16[64,384]{1,0:T(8,128)(2,1)} %get-tuple-element.9.refs_1_, bf16[384,1536]{1,0:T(8,128)(2,1)} %get-tuple-element.10.refs_2_, ...), custom_call_target="tpu_custom_call" | custom-call | bytes 4900000 | tf_op jit(solution)/shard_map/pallas_call | solution.py:645

commit v5 on v4

--- a/solution.py
+++ b/solution.py
@@ -575,13 +575,21 @@
 
 def settle(*refs):
     ins, outs, held, sems = refs[:4], refs[4:8], refs[8:12], refs[12]
-    loads = [pltpu.make_async_copy(ins[i], held[i], sems.at[0, i]) for i in range(4)]
-    stores = [pltpu.make_async_copy(held[i], outs[i], sems.at[1, i]) for i in range(4)]
-    for i in (2, 3, 0, 1):
-        loads[i].start()
-    for i in (2, 3, 0, 1):
-        loads[i].wait()
-        stores[i].start()
+    parts = [(i, pl.ds(n * rows, rows)) for n in range(4) for i, rows in ((2, 96), (3, 384))]
+    parts += [(0, pl.ds(0, 64)), (1, pl.ds(0, 64))]
+    loads = [
+        pltpu.make_async_copy(ins[i].at[at, :], held[i].at[at, :], sems.at[0, n])
+        for n, (i, at) in enumerate(parts)
+    ]
+    stores = [
+        pltpu.make_async_copy(held[i].at[at, :], outs[i].at[at, :], sems.at[1, n])
+        for n, (i, at) in enumerate(parts)
+    ]
+    for load in loads:
+        load.start()
+    for load, store in zip(loads, stores):
+        load.wait()
+        store.start()
     for store in stores:
         store.wait()
 
@@ -649,7 +657,7 @@
         out_specs=(hbm,) * 4,
         scratch_shapes=[
             *(pltpu.VMEM(shape.shape, BF) for shape in shapes),
-            dma((2, 4)),
+            dma((2, 10)),
         ],
         cost_estimate=pl.CostEstimate(
             flops=0, bytes_accessed=4_900_000, transcendentals=0

time: 110 us -> 110 us (level)
  no operation moved by 1% of the time
where the time goes in v5:
time: 110 us
  Pallas kernels  109 us (99%)
    pallas_call x1, Pallas kernels, shards(): pl.pallas_call(kernel, out_shape=shapes, in_specs=[hbm] * 4, out_specs=(v...  106 us
    pallas_call x1, Pallas kernels, shards(): pl.pallas_call(settle, out_shape=shapes, in_specs=[hbm] * 4, out_specs=(h...  2.55 us

profile of v5, /device:TPU:1, one launch (start us, length us, event | category | flops | bytes accessed | tf_op | source)
XLA Modules:
  0.0 109.8 jit_solution(14283421690830008766)
XLA Ops:
  0.6 106.5 %shard_map.75 = (bf16[64,384]{1,0:T(8,128)(2,1)}, bf16[64,384]{1,0:T(8,128)(2,1)}, bf16[384,1536]{1,0:T(8,128)(2,1)}, bf16[1536,384]{1,0:T(8,128)(2,1)}) custom-call(bf16[64,384]{1,0:T(8,128)(2,1)} %normed.1, bf16[384,1536]{1,0:T(8,128)(2,1)} %w_in.1, bf16[1536,384]{1,0:T(8,128)(2,1)} %w_out.1, bf16[64,384]{1,0:T(8,128)(2,1)} %cot.1), custom_call_target="tpu_custom_call" | custom-call | flops 7247757312 | bytes 5000000 | tf_op jit(solution)/shard_map/pallas_call | solution.py:607
  107.1 2.6 %shard_map.76 = (bf16[64,384]{1,0:T(8,128)(2,1)}, bf16[64,384]{1,0:T(8,128)(2,1)}, bf16[384,1536]{1,0:T(8,128)(2,1)}, bf16[1536,384]{1,0:T(8,128)(2,1)}) custom-call(bf16[64,384]{1,0:T(8,128)(2,1)} %get-tuple-element.8.refs_0_, bf16[64,384]{1,0:T(8,128)(2,1)} %get-tuple-element.9.refs_1_, bf16[384,1536]{1,0:T(8,128)(2,1)} %get-tuple-element.10.refs_2_, ...), custom_call_target="tpu_custom_call" | custom-call | bytes 4900000 | tf_op jit(solution)/shard_map/pallas_call | solution.py:653
